TPU v7x, 512 devices: a whole 4x4x16 slice. The times are simulated.
512 devices in a mesh: seq: 32 (over z, core), mp: 16 (over y, x).
Axes of the slice: x: 4, y: 4, z: 16, core: 2. Of those that a mesh axis runs over, the one named last changes fastest.
Arguments:
- residual: bfloat16 [4096, 8192], P('seq', 'mp'), may hold values from -6 to 6
- hyena_streams: bfloat16 [4096, 3, 8192], P('seq', None, 'mp'), may hold values from -6 to 6
- hyena_filter: float32 [7, 8192], P(None, 'mp'), may hold values from -3 to 3
- attention_streams: bfloat16 [4096, 3, 8192], P('seq', None, 'mp'), may hold values from -4.5 to 4.5
- norm_gain: float32 [8192], P('mp'), may hold values from 0.5 to 1.5
- record_starts: int32 [16], replicated, may hold values from 0 to 4095, as said below
- record_lengths: int32 [16], replicated, may hold values from 1 to 2048, as said below
- segment_ids: int32 [4096], P('seq'), may hold values from 0 to 15, as said below
Outputs:
- mixed: float32 [4096, 8192], P('seq', 'mp')
- record_energy: float32 [16], replicated
Inputs may be any that keep to these rules, and one draw needn't show every extreme that they name: Records lie end to end from position 0: record_starts[r] is the sum of record_lengths of the records before r, and they cover all 4096 positions; one record has exactly 2048 positions. record_starts[r] is the first position of record r, rising with r. segment_ids[t] is the record r with record_starts[r] <= t < record_starts[r] + record_lengths[r].
All inputs are finite; a program needn't handle non-finite values.
Results may differ from a plain program's by a relative error of at most 0.0005.
Values may be sent and summed in bfloat16 or wider, within the bound.
No kernel may reach another device: no remote copies, remote signals or barrier semaphores. Data moves between devices by JAX's collectives and lax.ppermute only.
A program may use at most 64 MiB of HBM per device.

v0:
```python
import jax
import jax.numpy as jnp
from jax import lax
from jax.sharding import PartitionSpec as P

D = 8192
HEAD_DIM = 128


def passed_along(value, axis, steps):
    count = lax.axis_size(axis)
    initial, last = (max(0, -steps), min(count, count - steps))
    return lax.ppermute(value, axis, [(source, source + steps) for source in range(initial, last)])


def on_device(
    residual,
    hyena_streams,
    hyena_filter,
    attention_streams,
    norm_gain,
    record_starts,
    record_lengths,
    segment_ids,
):
    rows = residual.shape[0]
    width = residual.shape[1]
    taps = hyena_filter.shape[0]
    records = record_starts.shape[0]
    positions = lax.axis_index("seq") * rows + jnp.arange(rows, dtype=jnp.int32)
    table = segment_ids[:, None] == jnp.arange(records, dtype=jnp.int32)[None, :]
    row_start = jnp.sum(jnp.where(table, record_starts[None, :], 0), axis=1)
    rim = passed_along(hyena_streams[rows - (taps - 1) :, 1:3, :], "seq", 1)
    product = hyena_streams[:, 1].astype(jnp.float32) * hyena_streams[:, 2].astype(jnp.float32)
    rim_product = rim[:, 0].astype(jnp.float32) * rim[:, 1].astype(jnp.float32)
    padded = jnp.concatenate([rim_product, product], axis=0)
    filtered = jnp.zeros((rows, width), jnp.float32)
    for tap in range(taps):
        term = padded[taps - 1 - tap : taps - 1 - tap + rows]
        valid = (positions - tap >= row_start)[:, None]
        filtered = filtered + jnp.where(valid, hyena_filter[tap][None, :] * term, jnp.float32(0.0))
    hyena_out = hyena_streams[:, 0].astype(jnp.float32) * filtered
    heads_here = width // HEAD_DIM
    scale = HEAD_DIM ** (-0.5)
    query = attention_streams[:, 0].reshape(rows, heads_here, HEAD_DIM)
    key_value = attention_streams[:, 1:3, :]
    lowest = jnp.min(row_start)
    highest = positions[rows - 1]

    def block_update(state, part, key_pos):
        running, totals, summed = state
        keys = part[:, 0].reshape(-1, heads_here, HEAD_DIM)
        values = part[:, 1].reshape(-1, heads_here, HEAD_DIM)
        allowed = (key_pos[None, :] <= positions[:, None]) & (
            key_pos[None, :] >= row_start[:, None]
        )
        scores = jnp.einsum("qhd,khd->hqk", query, keys, preferred_element_type=jnp.float32) * scale
        masked = jnp.where(allowed[None], scores, jnp.float32(-1e30))
        newest = jnp.maximum(running, jnp.max(masked, axis=2))
        factor = jnp.exp(running - newest)
        weights = jnp.where(allowed[None], jnp.exp(scores - newest[:, :, None]), jnp.float32(0.0))
        totals = totals * factor + jnp.sum(weights, axis=2)
        summed = summed * factor[:, :, None] + jnp.einsum(
            "hqk,khd->hqd", weights.astype(jnp.bfloat16), values, preferred_element_type=jnp.float32
        )
        return (newest, totals, summed)

    start_state = (
        jnp.full((heads_here, rows), -1e30, jnp.float32),
        jnp.zeros((heads_here, rows), jnp.float32),
        jnp.zeros((heads_here, rows, HEAD_DIM), jnp.float32),
    )
    carry = start_state
    piece = lax.all_gather(key_value, "seq", axis=0, tiled=True)
    start = jnp.int32(0)
    count = piece.shape[0]
    block = min(512, count)
    for first in range(0, count, block):
        part = piece[first : first + block]
        size_here = part.shape[0]
        key_first = start + first
        key_pos = key_first + jnp.arange(size_here, dtype=jnp.int32)
        needed = (key_first + size_here - 1 >= lowest) & (key_first <= highest)
        carry = lax.cond(
            needed, lambda state: block_update(state, part, key_pos), lambda state: state, carry
        )
    running, totals, summed = carry
    attention_out = (summed / totals[:, :, None]).transpose(1, 0, 2).reshape(rows, width)
    stream = residual.astype(jnp.float32) + hyena_out + attention_out
    squares = jnp.sum(stream * stream, axis=1)
    token_total = lax.psum(squares, "mp")
    mean_square = token_total / D
    local_sums = jnp.sum(jnp.where(table, mean_square[:, None], jnp.float32(0.0)), axis=0)
    record_sum = lax.psum(local_sums, "seq")
    mixed = stream * lax.rsqrt(mean_square + 1e-05)[:, None] * norm_gain[None, :]
    record_energy = record_sum / record_lengths.astype(jnp.float32)
    return (mixed, record_energy)


def solution(mesh):
    return jax.shard_map(
        on_device,
        mesh=mesh,
        in_specs=(
            P("seq", "mp"),
            P("seq", None, "mp"),
            P(None, "mp"),
            P("seq", None, "mp"),
            P("mp"),
            P(),
            P(),
            P("seq"),
        ),
        out_specs=(P("seq", "mp"), P()),
        check_vma=False,
    )
```

profile of v0, /device:TPU:1, one launch (start us, length us, event | category | flops | bytes accessed | tf_op | source)
XLA Modules:
  0.0 226.8 jit_solution(7465951158616911329)
XLA Ops:
  7.2 0.0 all-gather.2.cloned.1.call-start
  7.2 1.0 slice.160
  8.2 0.9 copy.90
  9.0 0.0 all-gather.2.cloned.1.call-update
  9.1 0.7 slice.145
  9.8 4.9 %collective-permute-start = (bf16[6,2,512]{2,0,1:T(8,128)(2,1)S(1)}, bf16[6,2,512]{2,0,1:T(8,128)(2,1)S(1)}, u32[]{:S(2)}, u32[]{:S(2)}) collective-permute-start(bf16[6,2,512]{2,0,1:T(8,128)(2,1)S(1)} %slice.145), channel_id=1, source_target_pairs={{0,16},{16,32},{32,48},{48,64},{64,80},{80,96},{96,112},{112,128},... | collective-permute-start | bytes 36872 | tf_op jit(solution)/shard_map/ppermute | solution.py:13
  14.7 0.5 iota_add_fusion.4
  15.3 0.6 iota_add_fusion.3
  15.9 0.6 iota_add_fusion.2
  16.5 0.6 iota_add_fusion.1
  17.0 0.8 select_reduce_fusion.9
  17.8 0.6 fusion.83
  18.4 1.6 fusion.94
  20.0 1.7 multiply_bitcast_fusion
  21.7 0.9 slice.162
  22.6 0.1 copy.91
  22.7 0.7 slice.159
  23.4 0.7 reduce_min.9
  34.5 0.0 collective-permute-done
  34.5 0.6 multiply_bitcast_fusion.1
  35.1 77.8 %all-gather.2.cloned.1.call-done = bf16[4096,2,512]{0,2,1:T(8,128)(2,1)} async-done(((bf16[128,2,512]{0,2,1:T(8,128)(2,1)}), bf16[4096,2,512]{0,2,1:T(8,128)(2,1)}) %all-gather.2.cloned.1.call-update) | async-done | bytes 8388624 | tf_op jit(solution)/shard_map/all_gather | solution.py:74
  112.9 4.6 %fusion.93 = (bf16[512,2,512]{0,2,1:T(8,128)(2,1)S(1)}, bf16[512,2,512]{0,2,1:T(8,128)(2,1)S(1)}, bf16[512,2,512]{0,2,1:T(8,128)(2,1)S(1)}, bf16[512,2,512]{0,2,...) fusion(bf16[4096,2,512]{0,2,1:T(8,128)(2,1)} %all-gather.2.cloned.1.call-done), kind=kLoop, calls=%fused_computation.176 | loop fusion | bytes 12582912 | tf_op jit(solution)/shard_map/slice | solution.py:79
  117.5 3.9 %conditional.8 = (f32[4,128]{1,0:T(4,128)}, f32[4,128]{1,0:T(4,128)S(1)}, f32[4,128,128]{2,1,0:T(8,128)S(1)}) conditional(s32[]{:T(128)} %convert_element_type.90, () %tuple.59, (s32[512]{0:T(512)S(1)}, s32[512]{0:T(512)S(1)}, s32[128]{0:T(128)S(1)}, s32[128]{0:T(128)S(1)}, bf16[512,2,512]{0,2,1:T(8,128)(2,1)S(1)}, ...), branch_computations={%region_2.3_spmd, %region_3.6_spmd} | conditional | flops 136841216 | bytes 6974488 | solution.py:84
  117.5 0.1 compare_and_fusion
  117.6 0.1 fusion.85
  117.7 0.5 select_reduce_fusion
  118.1 0.6 exponential_multiply_fusion
  118.7 1.0 fusion.1
  119.7 0.7 fusion.7
  120.4 1.0 convolution_add_fusion
  121.5 0.0 copy-start
  121.5 0.0 copy-start.1
  121.5 0.0 copy-start.2
  121.5 0.0 copy-start.3
  121.5 0.0 copy-start.4
  121.5 0.0 copy-start.5
  121.5 0.0 copy-start.6
  121.6 0.0 copy-start.7
  121.6 0.0 copy-start.8
  121.6 0.0 copy-start.9
  121.6 0.0 copy-start.11
  121.6 0.0 copy-start.12
  121.6 0.0 copy-start.13
  121.6 0.0 copy-start.14
  121.6 0.0 copy-start.15
  121.6 0.0 copy-start.16
  121.6 0.0 copy-start.17
  121.7 0.0 copy-start.18
  121.7 0.0 copy-start.19
  121.7 0.0 copy-start.10
  121.7 0.7 copy-done
  122.4 0.0 copy-done.1
  122.5 0.0 copy-done.2
  122.5 0.0 copy-done.3
  122.5 0.0 copy-done.4
  122.5 0.0 copy-done.5
  122.5 0.0 copy-done.6
  122.5 0.0 copy-done.7
  122.6 1.4 multiply_reduce_fusion
  124.0 33.0 %psum.14 = f32[128]{0:T(128)S(1)} all-reduce(f32[128]{0:T(128)S(1)} %get-tuple-element.449), channel_id=1, replica_groups=mesh['seq'=32,'mp'=16] {'mp'}, use_global_device_ids=true, to_apply=%region_35.36 | all-reduce | flops 128 | bytes 1024 | tf_op jit(solution)/shard_map/psum | solution.py:91
  157.0 0.1 select_reduce_fusion.8
  157.1 61.5 %psum.15 = f32[16]{0:T(128)S(1)} all-reduce(f32[16]{0:T(128)S(1)} %select_reduce_fusion.8), channel_id=1, replica_groups=mesh['seq'=32,'mp'=16] {'seq'}, use_global_device_ids=true, to_apply=%region_37.38 | all-reduce | flops 16 | bytes 128 | tf_op jit(solution)/shard_map/psum | solution.py:94
  218.6 0.5 convert_divide_fusion
  219.1 0.8 multiply_multiply_fusion
  (25 shorter events, 0.1 us)
Async XLA Ops:
  7.2 105.7 %all-gather.2.cloned.1.call-start = ((), (), s32[]{:S(2)}) async-start(), calls=%async_computation | async-start | bytes 8650752 | tf_op jit(solution)/shard_map/all_gather | solution.py:74
  9.8 24.7 %collective-permute-start = (bf16[6,2,512]{2,0,1:T(8,128)(2,1)S(1)}, bf16[6,2,512]{2,0,1:T(8,128)(2,1)S(1)}, u32[]{:S(2)}, u32[]{:S(2)}) collective-permute-start(bf16[6,2,512]{2,0,1:T(8,128)(2,1)S(1)} %slice.145), channel_id=1, source_target_pairs={{0,16},{16,32},{32,48},{48,64},{64,80},{80,96},{96,112},{112,128},... | collective-permute-start | bytes 36872 | tf_op jit(solution)/shard_map/ppermute | solution.py:13
  121.5 1.0 copy-start
  121.5 1.0 copy-start.1
  121.5 1.0 copy-start.2
  121.5 1.0 copy-start.3
  121.5 0.9 copy-start.4
  121.5 0.9 copy-start.5
  121.5 0.9 copy-start.6
  121.6 0.9 copy-start.7
  121.6 0.9 copy-start.8
  121.6 0.9 copy-start.9
  121.6 0.9 copy-start.11
  121.6 0.9 copy-start.12
  121.6 0.9 copy-start.13
  121.6 0.9 copy-start.14
  121.6 0.9 copy-start.15
  121.6 0.9 copy-start.16
  121.6 0.9 copy-start.17
  121.7 35.3 %copy-start.18 = (s32[128]{0:T(128)S(1)}, s32[128]{0:T(128)}, u32[]{:S(2)}) copy-start(s32[128]{0:T(128)} %param.31) | copy-start | bytes 1540
  121.7 96.9 %copy-start.19 = (s32[16]{0:T(128)S(1)}, s32[16]{0:T(128)}, u32[]{:S(2)}) copy-start(s32[16]{0:T(128)} %param.30) | copy-start | bytes 196
  121.7 97.4 %copy-start.10 = (f32[512]{0:T(512)S(1)}, f32[512]{0:T(512)}, u32[]{:S(2)}) copy-start(f32[512]{0:T(512)} %param.28) | copy-start | bytes 6148
Sparse Core Ops, SparseCore 0:
  10.0 102.7 all-gather.1
where the time goes:
time: 228 us; the launch traced here: 227 us
  blocking collectives  94.5 us (41%)
  waiting for transfers between devices  77.8 us (34%)
  between operations  24.8 us (11%)
  other arithmetic  11.9 us (5%)
  local copies, waits for them, and re-layouts  11.3 us (5%)
  starting transfers between devices  4.96 us (2%)
    all_gather x1, waiting for transfers between devices, on_device(): piece = lax.all_gather(key_value, 'seq', axis=0, tiled=True)  77.8 us
    psum x1, blocking collectives, on_device(): record_sum = lax.psum(local_sums, 'seq')  61.5 us
    psum x1, blocking collectives, on_device(): token_total = lax.psum(squares, 'mp')  33 us
    ppermute x1, starting transfers between devices, passed_along(): lax.ppermute(value, axis, [(source, source + steps) for source in range(i...  4.92 us
    slice x1, local copies, waits for them, and re-layouts, on_device(): part = piece[first:first + block]  4.6 us
  transfers between devices with their start and end apart: 2, of which 1 were waited for; matrix products, arithmetic and copies ran while one was open for 5% of the time, Pallas kernels for 0%

commit v1 on v0

v1 whole, which is shorter than its diff:
```python
import functools

import jax
import jax.numpy as jnp
from jax import lax
from jax.experimental import pallas as pl
from jax.experimental.pallas import tpu as pltpu
from jax.sharding import Mesh
from jax.sharding import PartitionSpec as P

D = 8192
HEAD_DIM = 128
GROUP = 4
GROUPS = 4
MASKED = -1e30
SCALE = HEAD_DIM**-0.5 * 1.4426950408889634
POSITIONS = ("zg", "zl", "core")


def pack_kernel(x_ref, out_ref):
    for head in range(GROUP):
        for stream in range(3):
            out_ref[head, stream] = x_ref[stream, :, head * HEAD_DIM : (head + 1) * HEAD_DIM]


def pack(streams):
    rows = streams.shape[1]
    return pl.pallas_call(
        pack_kernel,
        out_shape=jax.ShapeDtypeStruct((GROUP, 3, rows, HEAD_DIM), streams.dtype),
        name="pack_heads",
    )(streams)


def attend_kernel(back, first, last, scalars, starts, *refs):
    if first:
        q_ref, other_ref = refs[:2]
        own_ref, own_offset = q_ref, 1
        state_in, rest = None, refs[2:]
    else:
        q_ref, own_ref, other_ref = refs[:3]
        own_offset = 0
        state_in, rest = refs[3:6], refs[6:]
    group, core = scalars[0], scalars[1]
    rows = q_ref.shape[2]
    for block in range(GROUP):
        q = q_ref[block, 0]
        query_pos = ((group * GROUP + block) * 2 + core) * rows + lax.broadcasted_iota(
            jnp.int32, (rows, 1), 0
        )
        row_start = jnp.zeros((rows, 1), jnp.int32)
        for record in range(starts.shape[0]):
            here = starts[record]
            row_start = jnp.where(query_pos >= here, here, row_start)
        if back == 0:
            low, high = 0, block + 1
        elif back == 1:
            low, high = 0, GROUP
        else:
            low, high = block, GROUP
        count = (high - low) * rows
        scores = []
        sides = ((own_ref, own_offset, core), (other_ref, 0, 1 - core))
        for ref, offset, key_core in sides:
            keys = ref[low:high, offset].reshape(count, HEAD_DIM)
            s = lax.dot_general(q, keys, (((1,), (1,)), ((), ())), preferred_element_type=jnp.float32)
            place = lax.broadcasted_iota(jnp.int32, (1, count), 1)
            key_block = place // rows + low
            key_pos = (((group - back) * GROUP + key_block) * 2 + key_core) * rows + place % rows
            allowed = key_pos >= row_start
            if back == 0:
                allowed = allowed & (key_pos <= query_pos)
            scores.append(jnp.where(allowed, s * SCALE, MASKED))
        top = jnp.maximum(
            jnp.max(scores[0], axis=1, keepdims=True), jnp.max(scores[1], axis=1, keepdims=True)
        )
        if state_in is not None:
            top = jnp.maximum(top, state_in[0][block])
        total = jnp.zeros((rows, 1), jnp.float32)
        summed = jnp.zeros((rows, HEAD_DIM), jnp.float32)
        for s, (ref, offset, _) in zip(scores, sides):
            weights = jnp.exp2(s - top)
            total = total + jnp.sum(weights, axis=1, keepdims=True)
            values = ref[low:high, offset + 1].reshape(count, HEAD_DIM)
            summed = summed + jnp.dot(
                weights.astype(jnp.bfloat16), values, preferred_element_type=jnp.float32
            )
        if state_in is not None:
            factor = jnp.exp2(state_in[0][block] - top)
            total = total + state_in[1][block] * factor
            summed = summed + state_in[2][block] * factor
        if last:
            rest[0][block] = summed / total
        else:
            rest[0][block] = top
            rest[1][block] = total
            rest[2][block] = summed


def attend(back, scalars, starts, received, own, other, state):
    rows = received.shape[2]
    first, last = state is None, back == 2
    smem = pl.BlockSpec(memory_space=pltpu.SMEM)
    vmem = pl.BlockSpec(memory_space=pltpu.VMEM)
    column = jax.ShapeDtypeStruct((GROUP, rows, 1), jnp.float32)
    full = jax.ShapeDtypeStruct((GROUP, rows, HEAD_DIM), jnp.float32)
    operands = (scalars, starts, received) + ((other,) if first else (own, other) + tuple(state))
    out_shape = full if last else (column, column, full)
    return pl.pallas_call(
        functools.partial(attend_kernel, back, first, last),
        out_shape=out_shape,
        in_specs=[smem, smem] + [vmem] * (len(operands) - 2),
        out_specs=vmem if last else (vmem, vmem, vmem),
        compiler_params=pltpu.CompilerParams(vmem_limit_bytes=32 * 1024 * 1024),
        cost_estimate=pl.CostEstimate(
            flops=4 * GROUP * rows * GROUP * 2 * rows * HEAD_DIM,
            bytes_accessed=4 * 1024 * 1024,
            transcendentals=GROUP * rows * GROUP * 2 * rows,
        ),
        name=f"attend_back{back}",
    )(*operands)


def on_device(
    residual,
    hyena_streams,
    hyena_filter,
    attention_streams,
    norm_gain,
    record_starts,
    record_lengths,
    segment_ids,
):
    rows, width = residual.shape
    taps = hyena_filter.shape[0]
    records = record_starts.shape[0]
    group, core = lax.axis_index("zg"), lax.axis_index("core")
    scalars = jnp.stack([group, core]).astype(jnp.int32)

    with jax.named_scope("heads_to_chips"):
        packed = pack(attention_streams.transpose(1, 0, 2))
        received = lax.all_to_all(packed, "zl", 0, 0, tiled=True)
    key_value = received[:, 1:]
    swap = [(0, 1), (1, 0)]
    with jax.named_scope("keys_values_from_before"):
        before1 = lax.ppermute(key_value, "zg", [(i, i + 1) for i in range(GROUPS - 1)])
        before2 = lax.ppermute(key_value, "zg", [(i, i + 2) for i in range(GROUPS - 2)])
        other0 = lax.ppermute(key_value, "core", swap)
        other1 = lax.ppermute(before1, "core", swap)
        other2 = lax.ppermute(before2, "core", swap)

    with jax.named_scope("hyena"):
        edge, _ = lax.optimization_barrier((hyena_streams[rows - (taps - 1) :, 1:3, :], received))
        seq = lax.axis_size(POSITIONS)
        rim = lax.ppermute(edge, POSITIONS, [(i, i + 1) for i in range(seq - 1)])
        positions = lax.axis_index(POSITIONS) * rows + jnp.arange(rows, dtype=jnp.int32)
        table = segment_ids[:, None] == jnp.arange(records, dtype=jnp.int32)[None, :]
        row_start = jnp.sum(jnp.where(table, record_starts[None, :], 0), axis=1)
        product = hyena_streams[:, 1].astype(jnp.float32) * hyena_streams[:, 2].astype(jnp.float32)
        rim_product = rim[:, 0].astype(jnp.float32) * rim[:, 1].astype(jnp.float32)
        padded = jnp.concatenate([rim_product, product], axis=0)
        filtered = jnp.zeros((rows, width), jnp.float32)
        for tap in range(taps):
            term = padded[taps - 1 - tap : taps - 1 - tap + rows]
            valid = (positions - tap >= row_start)[:, None]
            filtered = filtered + jnp.where(
                valid, hyena_filter[tap][None, :] * term, jnp.float32(0.0)
            )
        hyena_out = hyena_streams[:, 0].astype(jnp.float32) * filtered
        base = residual.astype(jnp.float32) + hyena_out

    with jax.named_scope("attention"):
        state = attend(0, scalars, record_starts, received, None, other0, None)
        state = attend(1, scalars, record_starts, received, before1, other1, state)
        out = attend(2, scalars, record_starts, received, before2, other2, state)
        heads = lax.all_to_all(out, "zl", 0, 0, tiled=True)

    stream = base + heads.transpose(1, 0, 2).reshape(rows, width)
    with jax.named_scope("mean_square"):
        squares = jnp.sum(stream * stream, axis=1)
        size = lax.axis_size("mp")
        parts = lax.all_to_all(jnp.broadcast_to(squares, (size, 1, rows)), "mp", 0, 0, tiled=True)
        mean_square = jnp.sum(parts, axis=(0, 1)) / D
    mixed = stream * lax.rsqrt(mean_square + 1e-05)[:, None] * norm_gain[None, :]
    with jax.named_scope("record_energy"):
        local_sums = jnp.sum(jnp.where(table, mean_square[:, None], jnp.float32(0.0)), axis=0)
        parts = jnp.broadcast_to(jnp.pad(local_sums, (0, 128 - records)), (seq, 1, 128))
        parts = lax.all_to_all(parts, POSITIONS, 0, 0, tiled=True)
        record_sum = jnp.sum(parts, axis=(0, 1))[:records]
        record_energy = record_sum / record_lengths.astype(jnp.float32)
    return (mixed, record_energy)


def solution(mesh):
    fine = Mesh(
        mesh.devices.reshape(GROUPS, GROUP, 2, mesh.shape["mp"]), ("zg", "zl", "core", "mp")
    )
    return jax.shard_map(
        on_device,
        mesh=fine,
        in_specs=(
            P(POSITIONS, "mp"),
            P(POSITIONS, None, "mp"),
            P(None, "mp"),
            P(POSITIONS, None, "mp"),
            P("mp"),
            P(),
            P(),
            P(POSITIONS),
        ),
        out_specs=(P(POSITIONS, "mp"), P()),
        check_vma=False,
    )
```

time: 228 us -> 139 us (0.61)
  starting transfers between devices: 4.96 us -> 81.8 us
  blocking collectives: 94.5 us -> 27.2 us
  waiting for transfers between devices: 77.8 us -> 12.3 us
  between operations: 24.8 us -> 0.92 us
  other arithmetic: 11.9 us -> 2.53 us
  Pallas kernels: 0 us -> 9.22 us
  local copies, waits for them, and re-layouts: 11.3 us -> 4.44 us
    psum x2 -> x0, blocking collectives: 94.5 us -> none  [the longest x1 61.5 us: on_device(): record_sum = lax.psum(local_sums, 'seq')]
    all_gather x1 -> x0, waiting for transfers between devices: 77.8 us -> none  [on_device(): piece = lax.all_gather(key_value, 'seq', axis=0, tiled=True)]
    all_to_all x0 -> x2, starting transfers between devices: none -> 48.4 us  [the longest x1 24.8 us: on_device(): parts = lax.all_to_all(parts, POSITIONS, 0, 0, tiled=True)]
    ppermute x1 -> x6, starting transfers between devices: 4.92 us -> 33.4 us  [the longest x1 12 us: on_device(): lax.ppermute(key_value, 'zg', [(i, i + 1) for i in range(GROUPS - 1)])]
    all_to_all x0 -> x2, blocking collectives: none -> 27.2 us  [the longest x1 14.2 us: on_device(): received = lax.all_to_all(packed, 'zl', 0, 0, tiled=True)]
    all_to_all x0 -> x2, waiting for transfers between devices: none -> 10.1 us  [the longest x1 10.1 us: on_device(): parts = lax.all_to_all(parts, POSITIONS, 0, 0, tiled=True)]
    pallas_call x0 -> x4, Pallas kernels: none -> 9.22 us  [the longest x3 7.42 us: attend(): pl.pallas_call(functools.partial(attend_kernel, back, first, last), out_s...]
    slice x6 -> x3, local copies, waits for them, and re-layouts: 7.95 us -> 0.05 us  [the longest x1 0.03 us: on_device(): hyena_out = hyena_streams[:, 0].astype(jnp.float32) * filtered]
  transfers between devices with their start and end apart: 2 -> 8, of which waited for: 1 -> 2; matrix products, arithmetic and copies ran while one was open for 5% -> 1% of each run, Pallas kernels for 0% -> 3%
where the time goes in v1:
time: 139 us; the launch traced here: 138 us
  starting transfers between devices  81.8 us (59%)
  blocking collectives  27.2 us (20%)
  waiting for transfers between devices  12.3 us (9%)
  Pallas kernels  9.22 us (7%)
  local copies, waits for them, and re-layouts  4.44 us (3%)
  other arithmetic  2.53 us (2%)
    all_to_all x1, starting transfers between devices, on_device(): parts = lax.all_to_all(parts, POSITIONS, 0, 0, tiled=True)  24.8 us
    all_to_all x1, starting transfers between devices, on_device(): heads = lax.all_to_all(out, 'zl', 0, 0, tiled=True)  23.6 us
    all_to_all x1, blocking collectives, on_device(): received = lax.all_to_all(packed, 'zl', 0, 0, tiled=True)  14.2 us
    all_to_all x1, blocking collectives, on_device(): lax.all_to_all(jnp.broadcast_to(squares, (size, 1, rows)), 'mp', 0, 0, ti...  13 us
    ppermute x1, starting transfers between devices, on_device(): lax.ppermute(key_value, 'zg', [(i, i + 1) for i in range(GROUPS - 1)])  12 us
    all_to_all x1, waiting for transfers between devices, on_device(): parts = lax.all_to_all(parts, POSITIONS, 0, 0, tiled=True)  10.1 us
    ppermute x1, starting transfers between devices, on_device(): lax.ppermute(key_value, 'zg', [(i, i + 2) for i in range(GROUPS - 2)])  8.84 us
    pallas_call x3, Pallas kernels, attend(): pl.pallas_call(functools.partial(attend_kernel, back, first, last), out_s...  7.42 us
  transfers between devices with their start and end apart: 8, of which 2 were waited for; matrix products, arithmetic and copies ran while one was open for 1% of the time, Pallas kernels for 3%

profile of v1, /device:TPU:1, one launch (start us, length us, event | category | flops | bytes accessed | tf_op | source)
XLA Modules:
  0.0 138.4 jit_solution(11910158925160108408)
XLA Ops:
  0.6 1.8 %pack_heads.1 = bf16[4,3,128,128]{3,2,1,0:T(8,128)(2,1)} custom-call(bf16[3,128,512]{2,1,0:T(8,128)(2,1)} %bitcast.25), custom_call_target="tpu_custom_call" | custom-call | tf_op jit(solution)/shard_map/heads_to_chips/pack_heads/pallas_call | solution.py:28
  2.4 14.2 %all_to_all.20.refs_0_ = bf16[4,3,128,128]{3,2,1,0:T(8,128)(2,1)S(1)} all-to-all(bf16[4,3,128,128]{3,2,1,0:T(8,128)(2,1)} %pack_heads.1), channel_id=1, replica_groups=mesh['zg'=4,'zl'=4,'core'=2,'mp'=16] {'zl'}, dimensions={0} | all-to-all | bytes 786432 | tf_op jit(solution)/shard_map/heads_to_chips/all_to_all | solution.py:142
  16.6 0.0 copy-start.1
  16.6 12.0 %collective-permute-start.3 = (bf16[4,2,128,128]{3,2,1,0:T(8,128)(2,1)S(1)}, bf16[4,2,128,128]{3,2,1,0:T(8,128)(2,1)S(1)}, u32[]{:S(2)}, u32[]{:S(2)}) collective-permute-start(bf16[4,2,128,128]{3,2,1,0:T(8,128)(2,1)S(1)} %slice.96), channel_id=1, source_target_pairs={{0,128},{128,256},{256,384},{1,129},{129,257},{257,385},{2,130},{1... | collective-permute-start | bytes 786440 | tf_op jit(solution)/shard_map/keys_values_from_before/ppermute | solution.py:146
  28.7 8.8 %collective-permute-start.1 = (bf16[4,2,128,128]{3,2,1,0:T(8,128)(2,1)S(1)}, bf16[4,2,128,128]{3,2,1,0:T(8,128)(2,1)S(1)}, u32[]{:S(2)}, u32[]{:S(2)}) collective-permute-start(bf16[4,2,128,128]{3,2,1,0:T(8,128)(2,1)S(1)} %slice.96), channel_id=1, source_target_pairs={{0,256},{128,384},{1,257},{129,385},{2,258},{130,386},{3,259},{131... | collective-permute-start | bytes 786440 | tf_op jit(solution)/shard_map/keys_values_from_before/ppermute | solution.py:147
  37.5 0.0 copy-done.1
  37.6 3.9 %collective-permute-start.5 = (bf16[4,2,128,128]{3,2,1,0:T(8,128)(2,1)S(1)}, bf16[4,2,128,128]{3,2,1,0:T(8,128)(2,1)S(1)}, u32[]{:S(2)}, u32[]{:S(2)}) collective-permute-start(bf16[4,2,128,128]{3,2,1,0:T(8,128)(2,1)S(1)} %slice.96), channel_id=1, source_target_pairs={{0,16},{16,0},{1,17},{17,1},{2,18},{18,2},{3,19},{19,3},{4,20},{20... | collective-permute-start | bytes 786440 | tf_op jit(solution)/shard_map/keys_values_from_before/ppermute | solution.py:148
  41.5 0.0 collective-permute-done.3.refs_1_
  41.5 1.9 %collective-permute-start.4 = (bf16[4,2,128,128]{3,2,1,0:T(8,128)(2,1)S(1)}, bf16[4,2,128,128]{3,2,1,0:T(8,128)(2,1)S(1)}, u32[]{:S(2)}, u32[]{:S(2)}) collective-permute-start(bf16[4,2,128,128]{3,2,1,0:T(8,128)(2,1)S(1)} %collective-permute-done.3.refs_1_), channel_id=1, source_target_pairs={{0,16},{16,0},{1,17},{17,1},{2,18},{18,2},{3,19},{19,3},{4,20},{20... | collective-permute-start | bytes 786440 | tf_op jit(solution)/shard_map/keys_values_from_before/ppermute | solution.py:149
  43.4 0.1 pad_add_fusion.scalars
  43.5 0.1 copy.34
  43.6 0.1 copy.35
  43.8 0.0 copy-start.3
  43.8 0.2 copy.36
  44.0 0.0 copy-start
  44.0 0.0 collective-permute-done.1.refs_1_
  44.0 2.4 %collective-permute-start.2 = (bf16[4,2,128,128]{3,2,1,0:T(8,128)(2,1)S(1)}, bf16[4,2,128,128]{3,2,1,0:T(8,128)(2,1)S(1)}, u32[]{:S(2)}, u32[]{:S(2)}) collective-permute-start(bf16[4,2,128,128]{3,2,1,0:T(8,128)(2,1)S(1)} %collective-permute-done.1.refs_1_), channel_id=1, source_target_pairs={{0,16},{16,0},{1,17},{17,1},{2,18},{18,2},{3,19},{19,3},{4,20},{20... | collective-permute-start | bytes 786440 | tf_op jit(solution)/shard_map/keys_values_from_before/ppermute | solution.py:150
  46.4 0.0 copy-done.3
  46.5 0.0 collective-permute-done.5.refs_1_
  46.5 0.0 copy-done
  46.5 2.0 %attend_back0.1 = (f32[4,128,1]{2,1,0:T(8,128)S(1)}, f32[4,128,1]{2,1,0:T(8,128)S(1)}, f32[4,128,128]{2,1,0:T(8,128)S(1)}) custom-call(s32[2]{0:T(128)S(1)} %pad_add_fusion.scalars, s32[16]{0:T(128)S(1)} %copy-done, bf16[4,3,128,128]{3,2,1,0:T(8,128)(2,1)S(1)} %all_to_all.20.refs_0_, bf16[4,2,128,128]{3,2,1,0:T(8,128)(2,1)S(1)} %collective-permute-done.5.refs_1_), custom_call_target="tpu_custom_call" | custom-call | flops 268435456 | bytes 4194304 | tf_op jit(solution)/shard_map/attention/attend_back0/pallas_call | solution.py:109
  48.4 0.0 collective-permute-done.4.refs_2_
  48.5 2.5 %attend_back1.1 = (f32[4,128,1]{2,1,0:T(8,128)S(1)}, f32[4,128,1]{2,1,0:T(8,128)S(1)}, f32[4,128,128]{2,1,0:T(8,128)S(1)}) custom-call(s32[2]{0:T(128)S(1)} %pad_add_fusion.scalars, s32[16]{0:T(128)S(1)} %copy-done, bf16[4,3,128,128]{3,2,1,0:T(8,128)(2,1)S(1)} %all_to_all.20.refs_0_, bf16[4,2,128,128]{3,2,1,0:T(8,128)(2,1)S(1)} %collective-permute-done.3.refs_1_, ...), custom_call_target="tpu_custom_call" | custom-call | flops 268435456 | bytes 4194304 | tf_op jit(solution)/shard_map/attention/attend_back1/pallas_call | solution.py:109
  50.9 0.0 collective-permute-done.2.refs_2_
  50.9 3.0 %attend_back2.1 = f32[4,128,128]{2,1,0:T(8,128)} custom-call(s32[2]{0:T(128)S(1)} %pad_add_fusion.scalars, s32[16]{0:T(128)S(1)} %copy-done, bf16[4,3,128,128]{3,2,1,0:T(8,128)(2,1)S(1)} %all_to_all.20.refs_0_, bf16[4,2,128,128]{3,2,1,0:T(8,128)(2,1)S(1)} %collective-permute-done.1.refs_1_, bf16[4,2,128,128]{3,2,1,0:T(8,128)(2,1)S(1)} %collective-permute-done.2.refs_2_, ...), custom_call_target="tpu_custom_call" | custom-call | flops 268435456 | bytes 4194304 | tf_op jit(solution)/shard_map/attention/attend_back2/pallas_call | solution.py:109
  53.9 0.0 copy-start.5
  53.9 23.6 %all-to-all-start.1 = ((f32[4,128,128]{2,1,0:T(8,128)}), f32[4,128,128]{2,1,0:T(8,128)S(1)}, u32[]{:S(2)}, u32[]{:S(2)}) async-start(f32[4,128,128]{2,1,0:T(8,128)} %attend_back2.1), calls=%async_computation.1 | async-start | bytes 524288 | tf_op jit(solution)/shard_map/attention/all_to_all | solution.py:176
  77.6 0.0 copy-done.5
  77.6 0.1 select_reduce_fusion.1
  77.7 4.3 %collective-permute-start = (bf16[6,2,512]{0,2,1:T(8,128)(2,1)S(1)}, bf16[6,2,512]{0,2,1:T(8,128)(2,1)S(1)}, u32[]{:S(2)}, u32[]{:S(2)}) collective-permute-start(bf16[6,2,512]{0,2,1:T(8,128)(2,1)S(1)} %copy.36), channel_id=1, source_target_pairs={{0,16},{16,32},{32,48},{48,64},{64,80},{80,96},{96,112},{112,128},... | collective-permute-start | bytes 36872 | tf_op jit(solution)/shard_map/hyena/ppermute | solution.py:155
  82.0 0.0 copy-start.2
  82.0 0.1 copy.33
  82.2 0.8 copy-done.2
  82.9 0.1 copy.24
  83.1 2.3 %collective-permute-done = bf16[6,2,512]{0,2,1:T(8,128)(2,1)S(1)} collective-permute-done((bf16[6,2,512]{0,2,1:T(8,128)(2,1)S(1)}, bf16[6,2,512]{0,2,1:T(8,128)(2,1)S(1)}, u32[]{:S(2)}, u32[]{:S(2)}) %collective-permute-start) | collective-permute-done | bytes 12320 | tf_op jit(solution)/shard_map/hyena/ppermute | solution.py:155
  85.3 0.0 all-to-all-done.1
  85.4 0.1 copy.29
  85.5 1.5 %multiply_reduce_fusion = (f32[128]{0:T(128)S(1)}, f32[128,512]{0,1:T(8,128)S(1)}) fusion(f32[128,4,128]{0,2,1:T(8,128)S(1)} %copy.29, f32[128,512]{0,1:T(8,128)S(1)} %multiply_bitcast_fusion.1, f32[6,512]{0,1:T(8,128)S(1)} %multiply_bitcast_fusion, f32[512]{0:T(512)S(1)} %bitcast.33, pred[128]{0:T(512)(128)(4,1)S(1)} %get-tuple-element.37, ...), kind=kLoop, calls=%fused_computation.38 | loop fusion | flops 2162560 | bytes 1076608 | tf_op jit(solution)/shard_map/mean_square/reduce_sum | solution.py:180
  87.0 13.0 %all_to_all.21 = f32[16,1,128]{2,1,0:T(1,128)S(1)} all-to-all(f32[16,1,128]{2,1,0:T(1,128)S(1)} %broadcast_in_dim.101), channel_id=1, replica_groups=mesh['zg'=4,'zl'=4,'core'=2,'mp'=16] {'mp'}, dimensions={0} | all-to-all | bytes 16384 | tf_op jit(solution)/shard_map/mean_square/all_to_all | solution.py:182
  100.0 0.1 select_reduce_fusion
  100.1 0.6 broadcast_in_dim.104
  100.7 24.8 %all-to-all-start.3 = ((f32[32,1,128]{2,1,0:T(1,128)}), f32[32,1,128]{2,1,0:T(1,128)S(1)}, u32[]{:S(2)}, u32[]{:S(2)}) async-start(f32[32,1,128]{2,1,0:T(1,128)} %broadcast_in_dim.104), calls=%async_computation.3 | async-start | bytes 32768 | tf_op jit(solution)/shard_map/record_energy/all_to_all | solution.py:188
  125.5 0.0 copy-start.4
  125.5 0.7 copy-done.4
  126.2 0.1 multiply_multiply_fusion
  126.3 0.8 copy.32
  127.2 10.1 %all-to-all-done.3 = f32[32,1,128]{2,1,0:T(1,128)S(1)} async-done(((f32[32,1,128]{2,1,0:T(1,128)}), f32[32,1,128]{2,1,0:T(1,128)S(1)}, u32[]{:S(2)}, u32[]{:S(2)}) %all-to-all-start.3) | async-done | bytes 16416 | tf_op jit(solution)/shard_map/record_energy/all_to_all | solution.py:188
  137.2 0.0 copy-start.6
  137.3 0.6 copy-done.6
  137.9 0.5 convert_divide_fusion
  (12 shorter events, 0.2 us)
Async XLA Ops:
  16.6 20.9 %copy-start.1 = (bf16[128,3,512]{2,0,1:T(8,128)(2,1)S(1)}, bf16[128,3,512]{2,0,1:T(8,128)(2,1)}, u32[]{:S(2)}) copy-start(bf16[128,3,512]{2,0,1:T(8,128)(2,1)} %param.9) | copy-start | bytes 1179652
  16.6 24.8 %collective-permute-start.3 = (bf16[4,2,128,128]{3,2,1,0:T(8,128)(2,1)S(1)}, bf16[4,2,128,128]{3,2,1,0:T(8,128)(2,1)S(1)}, u32[]{:S(2)}, u32[]{:S(2)}) collective-permute-start(bf16[4,2,128,128]{3,2,1,0:T(8,128)(2,1)S(1)} %slice.96), channel_id=1, source_target_pairs={{0,128},{128,256},{256,384},{1,129},{129,257},{257,385},{2,130},{1... | collective-permute-start | bytes 786440 | tf_op jit(solution)/shard_map/keys_values_from_before/ppermute | solution.py:146
  28.7 15.3 %collective-permute-start.1 = (bf16[4,2,128,128]{3,2,1,0:T(8,128)(2,1)S(1)}, bf16[4,2,128,128]{3,2,1,0:T(8,128)(2,1)S(1)}, u32[]{:S(2)}, u32[]{:S(2)}) collective-permute-start(bf16[4,2,128,128]{3,2,1,0:T(8,128)(2,1)S(1)} %slice.96), channel_id=1, source_target_pairs={{0,256},{128,384},{1,257},{129,385},{2,258},{130,386},{3,259},{131... | collective-permute-start | bytes 786440 | tf_op jit(solution)/shard_map/keys_values_from_before/ppermute | solution.py:147
  37.6 8.9 %collective-permute-start.5 = (bf16[4,2,128,128]{3,2,1,0:T(8,128)(2,1)S(1)}, bf16[4,2,128,128]{3,2,1,0:T(8,128)(2,1)S(1)}, u32[]{:S(2)}, u32[]{:S(2)}) collective-permute-start(bf16[4,2,128,128]{3,2,1,0:T(8,128)(2,1)S(1)} %slice.96), channel_id=1, source_target_pairs={{0,16},{16,0},{1,17},{17,1},{2,18},{18,2},{3,19},{19,3},{4,20},{20... | collective-permute-start | bytes 786440 | tf_op jit(solution)/shard_map/keys_values_from_before/ppermute | solution.py:148
  41.5 7.0 %collective-permute-start.4 = (bf16[4,2,128,128]{3,2,1,0:T(8,128)(2,1)S(1)}, bf16[4,2,128,128]{3,2,1,0:T(8,128)(2,1)S(1)}, u32[]{:S(2)}, u32[]{:S(2)}) collective-permute-start(bf16[4,2,128,128]{3,2,1,0:T(8,128)(2,1)S(1)} %collective-permute-done.3.refs_1_), channel_id=1, source_target_pairs={{0,16},{16,0},{1,17},{17,1},{2,18},{18,2},{3,19},{19,3},{4,20},{20... | collective-permute-start | bytes 786440 | tf_op jit(solution)/shard_map/keys_values_from_before/ppermute | solution.py:149
  43.8 2.7 %copy-start.3 = (f32[7,512]{1,0:T(8,128)S(1)}, f32[7,512]{1,0:T(8,128)}, u32[]{:S(2)}) copy-start(f32[7,512]{1,0:T(8,128)} %param.10) | copy-start | bytes 43012
  44.0 2.5 %copy-start = (s32[16]{0:T(128)S(1)}, s32[16]{0:T(128)}, u32[]{:S(2)}) copy-start(s32[16]{0:T(128)} %starts.5) | copy-start | bytes 196
  44.0 6.9 %collective-permute-start.2 = (bf16[4,2,128,128]{3,2,1,0:T(8,128)(2,1)S(1)}, bf16[4,2,128,128]{3,2,1,0:T(8,128)(2,1)S(1)}, u32[]{:S(2)}, u32[]{:S(2)}) collective-permute-start(bf16[4,2,128,128]{3,2,1,0:T(8,128)(2,1)S(1)} %collective-permute-done.1.refs_1_), channel_id=1, source_target_pairs={{0,16},{16,0},{1,17},{17,1},{2,18},{18,2},{3,19},{19,3},{4,20},{20... | collective-permute-start | bytes 786440 | tf_op jit(solution)/shard_map/keys_values_from_before/ppermute | solution.py:150
  53.9 23.6 %copy-start.5 = (s32[128]{0:T(128)S(1)}, s32[128]{0:T(128)}, u32[]{:S(2)}) copy-start(s32[128]{0:T(128)} %param.15) | copy-start | bytes 1540
  53.9 31.4 %all-to-all-start.1 = ((f32[4,128,128]{2,1,0:T(8,128)}), f32[4,128,128]{2,1,0:T(8,128)S(1)}, u32[]{:S(2)}, u32[]{:S(2)}) async-start(f32[4,128,128]{2,1,0:T(8,128)} %attend_back2.1), calls=%async_computation.1 | async-start | bytes 524288 | tf_op jit(solution)/shard_map/attention/all_to_all | solution.py:176
  77.7 7.6 %collective-permute-start = (bf16[6,2,512]{0,2,1:T(8,128)(2,1)S(1)}, bf16[6,2,512]{0,2,1:T(8,128)(2,1)S(1)}, u32[]{:S(2)}, u32[]{:S(2)}) collective-permute-start(bf16[6,2,512]{0,2,1:T(8,128)(2,1)S(1)} %copy.36), channel_id=1, source_target_pairs={{0,16},{16,32},{32,48},{48,64},{64,80},{80,96},{96,112},{112,128},... | collective-permute-start | bytes 36872 | tf_op jit(solution)/shard_map/hyena/ppermute | solution.py:155
  82.0 0.9 copy-start.2
  100.7 36.5 %all-to-all-start.3 = ((f32[32,1,128]{2,1,0:T(1,128)}), f32[32,1,128]{2,1,0:T(1,128)S(1)}, u32[]{:S(2)}, u32[]{:S(2)}) async-start(f32[32,1,128]{2,1,0:T(1,128)} %broadcast_in_dim.104), calls=%async_computation.3 | async-start | bytes 32768 | tf_op jit(solution)/shard_map/record_energy/all_to_all | solution.py:188
  125.5 0.7 copy-start.4
  137.2 0.7 copy-start.6

commit v2 on v1

--- a/solution.py
+++ b/solution.py
@@ -48,10 +48,7 @@
         query_pos = ((group * GROUP + block) * 2 + core) * rows + lax.broadcasted_iota(
             jnp.int32, (rows, 1), 0
         )
-        row_start = jnp.zeros((rows, 1), jnp.int32)
-        for record in range(starts.shape[0]):
-            here = starts[record]
-            row_start = jnp.where(query_pos >= here, here, row_start)
+        row_start = row_starts(starts, query_pos)
         if back == 0:
             low, high = 0, block + 1
         elif back == 1:
@@ -112,13 +109,73 @@
         in_specs=[smem, smem] + [vmem] * (len(operands) - 2),
         out_specs=vmem if last else (vmem, vmem, vmem),
         compiler_params=pltpu.CompilerParams(vmem_limit_bytes=32 * 1024 * 1024),
-        cost_estimate=pl.CostEstimate(
-            flops=4 * GROUP * rows * GROUP * 2 * rows * HEAD_DIM,
-            bytes_accessed=4 * 1024 * 1024,
-            transcendentals=GROUP * rows * GROUP * 2 * rows,
-        ),
+        cost_estimate=cost(2500),
         name=f"attend_back{back}",
     )(*operands)
+
+
+def row_starts(starts, positions):
+    found = jnp.zeros_like(positions)
+    for record in range(starts.shape[0]):
+        here = starts[record]
+        found = jnp.where(positions >= here, here, found)
+    return found
+
+
+def hyena_kernel(scalars, starts, residual, streams, rim, taps_ref, out_ref, padded):
+    rows = residual.shape[0]
+    edge = rim.shape[1]
+    taps = taps_ref.shape[0]
+    positions = scalars[2] * rows + lax.broadcasted_iota(jnp.int32, (rows, 1), 0)
+    first = row_starts(starts, positions)
+    padded[:edge] = rim[0].astype(jnp.float32) * rim[1].astype(jnp.float32)
+    padded[edge:] = streams[1].astype(jnp.float32) * streams[2].astype(jnp.float32)
+    filtered = jnp.zeros(out_ref.shape, jnp.float32)
+    for tap in range(taps):
+        term = taps_ref[tap : tap + 1, :] * padded[edge - tap : edge - tap + rows]
+        filtered = filtered + jnp.where(positions - tap >= first, term, 0.0)
+    out_ref[...] = residual[...].astype(jnp.float32) + streams[0].astype(jnp.float32) * filtered
+
+
+def stream_kernel(base, heads, stream_ref, squares_ref):
+    rows = base.shape[0]
+    squares = jnp.zeros((rows, HEAD_DIM), jnp.float32)
+    for head in range(GROUP):
+        columns = slice(head * HEAD_DIM, (head + 1) * HEAD_DIM)
+        value = base[:, columns] + heads[head]
+        stream_ref[:, columns] = value
+        squares = squares + value * value
+    line = jnp.sum(squares.T, axis=0, keepdims=True)
+    for device in range(squares_ref.shape[0]):
+        squares_ref[device] = line
+
+
+def records_kernel(scalars, starts, lengths, parts, mean_ref, sums_ref):
+    rows = parts.shape[2]
+    line = jnp.sum(parts[:, 0, :], axis=0, keepdims=True) / D
+    mean = jnp.broadcast_to(line, (rows, rows)).T
+    mean_ref[...] = mean
+    position = scalars[2] * rows + lax.broadcasted_iota(jnp.int32, (rows, rows), 0)
+    first = starts[...]
+    inside = (position >= first) & (position < first + lengths[...])
+    sums = jnp.sum(jnp.where(inside, mean, 0.0), axis=0, keepdims=True)
+    for device in range(sums_ref.shape[0]):
+        sums_ref[device] = sums
+
+
+def scale_kernel(stream, mean, gain, out_ref):
+    factor = lax.rsqrt(mean[...] + 1e-05)
+    for head in range(GROUP):
+        columns = slice(head * HEAD_DIM, (head + 1) * HEAD_DIM)
+        out_ref[:, columns] = stream[:, columns] * factor * gain[:, columns]
+
+
+SMEM = pl.BlockSpec(memory_space=pltpu.SMEM)
+VMEM = pl.BlockSpec(memory_space=pltpu.VMEM)
+
+
+def cost(nanoseconds):
+    return pl.CostEstimate(flops=nanoseconds * 1_000_000, bytes_accessed=1 << 20, transcendentals=0)
 
 
 def on_device(
@@ -132,10 +189,10 @@
     segment_ids,
 ):
     rows, width = residual.shape
-    taps = hyena_filter.shape[0]
     records = record_starts.shape[0]
     group, core = lax.axis_index("zg"), lax.axis_index("core")
-    scalars = jnp.stack([group, core]).astype(jnp.int32)
+    seq, mp = lax.axis_size(POSITIONS), lax.axis_size("mp")
+    scalars = jnp.stack([group, core, lax.axis_index(POSITIONS)]).astype(jnp.int32)
 
     with jax.named_scope("heads_to_chips"):
         packed = pack(attention_streams.transpose(1, 0, 2))
@@ -147,47 +204,58 @@
         before2 = lax.ppermute(key_value, "zg", [(i, i + 2) for i in range(GROUPS - 2)])
         other0 = lax.ppermute(key_value, "core", swap)
         other1 = lax.ppermute(before1, "core", swap)
-        other2 = lax.ppermute(before2, "core", swap)
 
     with jax.named_scope("hyena"):
-        edge, _ = lax.optimization_barrier((hyena_streams[rows - (taps - 1) :, 1:3, :], received))
-        seq = lax.axis_size(POSITIONS)
+        streams = hyena_streams.transpose(1, 0, 2)
+        edge, _ = lax.optimization_barrier((streams[1:, rows - 16 :], other0))
         rim = lax.ppermute(edge, POSITIONS, [(i, i + 1) for i in range(seq - 1)])
-        positions = lax.axis_index(POSITIONS) * rows + jnp.arange(rows, dtype=jnp.int32)
-        table = segment_ids[:, None] == jnp.arange(records, dtype=jnp.int32)[None, :]
-        row_start = jnp.sum(jnp.where(table, record_starts[None, :], 0), axis=1)
-        product = hyena_streams[:, 1].astype(jnp.float32) * hyena_streams[:, 2].astype(jnp.float32)
-        rim_product = rim[:, 0].astype(jnp.float32) * rim[:, 1].astype(jnp.float32)
-        padded = jnp.concatenate([rim_product, product], axis=0)
-        filtered = jnp.zeros((rows, width), jnp.float32)
-        for tap in range(taps):
-            term = padded[taps - 1 - tap : taps - 1 - tap + rows]
-            valid = (positions - tap >= row_start)[:, None]
-            filtered = filtered + jnp.where(
-                valid, hyena_filter[tap][None, :] * term, jnp.float32(0.0)
-            )
-        hyena_out = hyena_streams[:, 0].astype(jnp.float32) * filtered
-        base = residual.astype(jnp.float32) + hyena_out
+        base = pl.pallas_call(
+            hyena_kernel,
+            out_shape=jax.ShapeDtypeStruct((rows, width), jnp.float32),
+            in_specs=[SMEM, SMEM, VMEM, VMEM, VMEM, VMEM],
+            out_specs=VMEM,
+            scratch_shapes=[pltpu.VMEM((rows + 16, width), jnp.float32)],
+            cost_estimate=cost(1500),
+            name="hyena",
+        )(scalars, record_starts, residual, streams, rim, hyena_filter)
 
     with jax.named_scope("attention"):
         state = attend(0, scalars, record_starts, received, None, other0, None)
+        before2, base, state = lax.optimization_barrier((before2, base, state))
+        other2 = lax.ppermute(before2, "core", swap)
         state = attend(1, scalars, record_starts, received, before1, other1, state)
         out = attend(2, scalars, record_starts, received, before2, other2, state)
         heads = lax.all_to_all(out, "zl", 0, 0, tiled=True)
 
-    stream = base + heads.transpose(1, 0, 2).reshape(rows, width)
     with jax.named_scope("mean_square"):
-        squares = jnp.sum(stream * stream, axis=1)
-        size = lax.axis_size("mp")
-        parts = lax.all_to_all(jnp.broadcast_to(squares, (size, 1, rows)), "mp", 0, 0, tiled=True)
-        mean_square = jnp.sum(parts, axis=(0, 1)) / D
-    mixed = stream * lax.rsqrt(mean_square + 1e-05)[:, None] * norm_gain[None, :]
+        stream, squares = pl.pallas_call(
+            stream_kernel,
+            out_shape=(
+                jax.ShapeDtypeStruct((rows, width), jnp.float32),
+                jax.ShapeDtypeStruct((mp, 1, rows), jnp.float32),
+            ),
+            name="stream",
+        )(base, heads)
+        parts = lax.all_to_all(squares, "mp", 0, 0, tiled=True)
     with jax.named_scope("record_energy"):
-        local_sums = jnp.sum(jnp.where(table, mean_square[:, None], jnp.float32(0.0)), axis=0)
-        parts = jnp.broadcast_to(jnp.pad(local_sums, (0, 128 - records)), (seq, 1, 128))
-        parts = lax.all_to_all(parts, POSITIONS, 0, 0, tiled=True)
-        record_sum = jnp.sum(parts, axis=(0, 1))[:records]
-        record_energy = record_sum / record_lengths.astype(jnp.float32)
+        lines = [jnp.pad(x, (0, 128 - records))[None, :] for x in (record_starts, record_lengths)]
+        mean, sums = pl.pallas_call(
+            records_kernel,
+            out_shape=(
+                jax.ShapeDtypeStruct((rows, rows), jnp.float32),
+                jax.ShapeDtypeStruct((seq, 1, 128), jnp.float32),
+            ),
+            in_specs=[SMEM, VMEM, VMEM, VMEM],
+            name="records",
+        )(scalars, *lines, parts)
+        sums = lax.all_to_all(sums, POSITIONS, 0, 0, tiled=True)
+        record_energy = jnp.sum(sums, axis=(0, 1))[:records] / record_lengths.astype(jnp.float32)
+    mixed = pl.pallas_call(
+        scale_kernel,
+        out_shape=jax.ShapeDtypeStruct((rows, width), jnp.float32),
+        cost_estimate=cost(1000),
+        name="scale",
+    )(stream, mean, norm_gain[None, :])
     return (mixed, record_energy)
 
 

time: 139 us -> 144 us (1.036)
  blocking collectives: 27.2 us -> 14.2 us
  waiting for transfers between devices: 12.3 us -> 22.6 us
  Pallas kernels: 9.22 us -> 16.6 us
  starting transfers between devices: 81.8 us -> 85.2 us
  other arithmetic: 2.53 us -> 0.65 us
    all_to_all x1 -> x0, blocking collectives: 13 us -> none  [on_device(): lax.all_to_all(jnp.broadcast_to(squares, (size, 1, rows)), 'mp', 0, 0, ti...]
    pallas_call x0 -> x4, Pallas kernels: none -> 7.34 us  [the longest x1 2.29 us: on_device(): pl.pallas_call(hyena_kernel, out_shape=jax.ShapeDtypeStruct((rows, width)...]
    all_to_all x1, waiting for transfers between devices: 0.01 us -> 6.88 us  [on_device(): heads = lax.all_to_all(out, 'zl', 0, 0, tiled=True)]
    all_to_all x1 -> x2, waiting for transfers between devices: 10.1 us -> 15.7 us  [the longest x1 10 us: on_device(): sums = lax.all_to_all(sums, POSITIONS, 0, 0, tiled=True)]
    all_to_all x1 -> x2, starting transfers between devices: 24.8 us -> 29.7 us  [the longest x1 22.8 us: on_device(): sums = lax.all_to_all(sums, POSITIONS, 0, 0, tiled=True)]
    ppermute x1, starting transfers between devices: 12 us -> 8.72 us  [on_device(): lax.ppermute(key_value, 'zg', [(i, i + 1) for i in range(GROUPS - 1)])]
    ppermute x1, starting transfers between devices: 3.88 us -> 6.9 us  [on_device(): other0 = lax.ppermute(key_value, 'core', swap)]
    ppermute x1, waiting for transfers between devices: 2.25 us -> 0.01 us  [on_device(): rim = lax.ppermute(edge, POSITIONS, [(i, i + 1) for i in range(seq - 1)])]
  transfers between devices with their start and end apart: 8 -> 9, of which waited for: 2 -> 3; matrix products, arithmetic and copies ran while one was open for 1% -> 1% of each run, Pallas kernels for 3% -> 6%
where the time goes in v2:
time: 144 us
  starting transfers between devices  85.2 us (59%)
  waiting for transfers between devices  22.6 us (16%)
  Pallas kernels  16.6 us (12%)
  blocking collectives  14.2 us (10%)
  local copies, waits for them, and re-layouts  3.79 us (3%)
    all_to_all x1, starting transfers between devices, on_device(): heads = lax.all_to_all(out, 'zl', 0, 0, tiled=True)  24.7 us
    all_to_all x1, starting transfers between devices, on_device(): sums = lax.all_to_all(sums, POSITIONS, 0, 0, tiled=True)  22.8 us
    all_to_all x1, blocking collectives, on_device(): received = lax.all_to_all(packed, 'zl', 0, 0, tiled=True)  14.2 us
    all_to_all x1, waiting for transfers between devices, on_device(): sums = lax.all_to_all(sums, POSITIONS, 0, 0, tiled=True)  10 us
    ppermute x1, starting transfers between devices, on_device(): lax.ppermute(key_value, 'zg', [(i, i + 1) for i in range(GROUPS - 1)])  8.72 us
    ppermute x1, starting transfers between devices, on_device(): lax.ppermute(key_value, 'zg', [(i, i + 2) for i in range(GROUPS - 2)])  8.44 us
    pallas_call x3, Pallas kernels, attend(): pl.pallas_call(functools.partial(attend_kernel, back, first, last), out_s...  7.4 us
    ppermute x1, starting transfers between devices, on_device(): other0 = lax.ppermute(key_value, 'core', swap)  6.9 us
  transfers between devices with their start and end apart: 9, of which 3 were waited for; matrix products, arithmetic and copies ran while one was open for 1% of the time, Pallas kernels for 6%

profile of v2, /device:TPU:1, one launch (start us, length us, event | category | flops | bytes accessed | tf_op | source)
XLA Modules:
  0.0 143.8 jit_solution(9683816263494034139)
XLA Ops:
  0.6 1.8 %pack_heads.1 = bf16[4,3,128,128]{3,2,1,0:T(8,128)(2,1)} custom-call(bf16[3,128,512]{2,1,0:T(8,128)(2,1)} %bitcast.10), custom_call_target="tpu_custom_call" | custom-call | tf_op jit(solution)/shard_map/heads_to_chips/pack_heads/pallas_call | solution.py:28
  2.4 14.2 %all_to_all.20.refs_0_ = bf16[4,3,128,128]{3,2,1,0:T(8,128)(2,1)S(1)} all-to-all(bf16[4,3,128,128]{3,2,1,0:T(8,128)(2,1)} %pack_heads.1), channel_id=1, replica_groups=mesh['zg'=4,'zl'=4,'core'=2,'mp'=16] {'zl'}, dimensions={0} | all-to-all | bytes 786432 | tf_op jit(solution)/shard_map/heads_to_chips/all_to_all | solution.py:199
  16.7 6.9 %collective-permute-start.1 = (bf16[4,2,128,128]{3,2,1,0:T(8,128)(2,1)S(1)}, bf16[4,2,128,128]{3,2,1,0:T(8,128)(2,1)S(1)}, u32[]{:S(2)}, u32[]{:S(2)}) collective-permute-start(bf16[4,2,128,128]{3,2,1,0:T(8,128)(2,1)S(1)} %slice.12), channel_id=1, source_target_pairs={{0,16},{16,0},{1,17},{17,1},{2,18},{18,2},{3,19},{19,3},{4,20},{20... | collective-permute-start | bytes 786440 | tf_op jit(solution)/shard_map/keys_values_from_before/ppermute | solution.py:205
  23.6 8.7 %collective-permute-start.4 = (bf16[4,2,128,128]{3,2,1,0:T(8,128)(2,1)S(1)}, bf16[4,2,128,128]{3,2,1,0:T(8,128)(2,1)S(1)}, u32[]{:S(2)}, u32[]{:S(2)}) collective-permute-start(bf16[4,2,128,128]{3,2,1,0:T(8,128)(2,1)S(1)} %slice.12), channel_id=1, source_target_pairs={{0,128},{128,256},{256,384},{1,129},{129,257},{257,385},{2,130},{1... | collective-permute-start | bytes 786440 | tf_op jit(solution)/shard_map/keys_values_from_before/ppermute | solution.py:203
  32.3 0.8 slice.13
  33.1 0.0 copy-start.2
  33.1 0.1 pad_add_fusion.scalars
  33.2 0.0 copy-start
  33.2 8.4 %collective-permute-start = (bf16[4,2,128,128]{3,2,1,0:T(8,128)(2,1)S(1)}, bf16[4,2,128,128]{3,2,1,0:T(8,128)(2,1)S(1)}, u32[]{:S(2)}, u32[]{:S(2)}) collective-permute-start(bf16[4,2,128,128]{3,2,1,0:T(8,128)(2,1)S(1)} %slice.12), channel_id=1, source_target_pairs={{0,256},{128,384},{1,257},{129,385},{2,258},{130,386},{3,259},{131... | collective-permute-start | bytes 786440 | tf_op jit(solution)/shard_map/keys_values_from_before/ppermute | solution.py:204
  41.6 0.0 collective-permute-done.1.refs_1_
  41.6 2.3 %collective-permute-start.2 = (bf16[2,16,512]{2,1,0:T(8,128)(2,1)S(1)}, bf16[2,16,512]{2,1,0:T(8,128)(2,1)S(1)}, u32[]{:S(2)}, u32[]{:S(2)}) collective-permute-start(bf16[2,16,512]{2,1,0:T(8,128)(2,1)S(1)} %slice.13), channel_id=1, source_target_pairs={{0,16},{16,32},{32,48},{48,64},{64,80},{80,96},{96,112},{112,128},... | collective-permute-start | bytes 98312 | tf_op jit(solution)/shard_map/hyena/ppermute | solution.py:211
  43.9 0.0 collective-permute-done.4.refs_1_
  43.9 2.0 %collective-permute-start.5 = (bf16[4,2,128,128]{3,2,1,0:T(8,128)(2,1)S(1)}, bf16[4,2,128,128]{3,2,1,0:T(8,128)(2,1)S(1)}, u32[]{:S(2)}, u32[]{:S(2)}) collective-permute-start(bf16[4,2,128,128]{3,2,1,0:T(8,128)(2,1)S(1)} %collective-permute-done.4.refs_1_), channel_id=1, source_target_pairs={{0,16},{16,0},{1,17},{17,1},{2,18},{18,2},{3,19},{19,3},{4,20},{20... | collective-permute-start | bytes 786440 | tf_op jit(solution)/shard_map/keys_values_from_before/ppermute | solution.py:206
  46.0 0.0 copy-done.2
  46.0 2.0 %attend_back0.1 = (f32[4,128,1]{2,1,0:T(8,128)S(1)}, f32[4,128,1]{2,1,0:T(8,128)S(1)}, f32[4,128,128]{2,1,0:T(8,128)S(1)}) custom-call(s32[3]{0:T(128)S(1)} %pad_add_fusion.scalars, s32[16]{0:T(128)S(1)} %copy-done.2, bf16[4,3,128,128]{3,2,1,0:T(8,128)(2,1)S(1)} %all_to_all.20.refs_0_, bf16[4,2,128,128]{3,2,1,0:T(8,128)(2,1)S(1)} %collective-permute-done.1.refs_1_), custom_call_target="tpu_custom_call" | custom-call | flops 2500000000 | bytes 1048576 | tf_op jit(solution)/shard_map/attention/attend_back0/pallas_call | solution.py:106
  47.9 0.0 copy-done
  47.9 0.0 collective-permute-done.2.rim
  48.0 0.0 copy-start.6
  48.0 0.6 copy-done.6
  48.6 2.3 %hyena.1.base = f32[128,512]{1,0:T(8,128)} custom-call(s32[3]{0:T(128)} %copy-done, s32[16]{0:T(128)} %starts.7, bf16[128,512]{1,0:T(8,128)(2,1)} %residual.1, bf16[3,128,512]{2,1,0:T(8,128)(2,1)} %bitcast.12, bf16[2,16,512]{2,1,0:T(8,128)(2,1)} %copy-done.6, f32[7,512]{1,0:T(8,128)} %taps_ref.1), custom_call_target="tpu_custom_call" | custom-call | flops 1500000000 | bytes 1048576 | tf_op jit(solution)/shard_map/hyena/hyena/pallas_call | solution.py:212
  50.9 0.0 collective-permute-done.refs_1_
  50.9 0.0 copy-start.1
  50.9 0.0 copy-start.3
  50.9 2.4 %collective-permute-start.3 = (bf16[4,2,128,128]{3,2,1,0:T(8,128)(2,1)S(1)}, bf16[4,2,128,128]{3,2,1,0:T(8,128)(2,1)S(1)}, u32[]{:S(2)}, u32[]{:S(2)}) collective-permute-start(bf16[4,2,128,128]{3,2,1,0:T(8,128)(2,1)S(1)} %collective-permute-done.refs_1_), channel_id=1, source_target_pairs={{0,16},{16,0},{1,17},{17,1},{2,18},{18,2},{3,19},{19,3},{4,20},{20... | collective-permute-start | bytes 786440 | tf_op jit(solution)/shard_map/attention/ppermute | solution.py:225
  53.3 0.0 collective-permute-done.5.refs_2_
  53.3 0.0 copy-done.1
  53.3 0.0 copy-done.3
  53.3 2.5 %attend_back1.1 = (f32[4,128,1]{2,1,0:T(8,128)S(1)}, f32[4,128,1]{2,1,0:T(8,128)S(1)}, f32[4,128,128]{2,1,0:T(8,128)S(1)}) custom-call(s32[3]{0:T(128)S(1)} %copy-done.1, s32[16]{0:T(128)S(1)} %copy-done.3, bf16[4,3,128,128]{3,2,1,0:T(8,128)(2,1)S(1)} %all_to_all.20.refs_0_, bf16[4,2,128,128]{3,2,1,0:T(8,128)(2,1)S(1)} %collective-permute-done.4.refs_1_, ...), custom_call_target="tpu_custom_call" | custom-call | flops 2500000000 | bytes 1048576 | tf_op jit(solution)/shard_map/attention/attend_back1/pallas_call | solution.py:106
  55.8 0.0 collective-permute-done.3.refs_2_
  55.8 3.0 %attend_back2.1 = f32[4,128,128]{2,1,0:T(8,128)} custom-call(s32[3]{0:T(128)S(1)} %copy-done.1, s32[16]{0:T(128)S(1)} %copy-done.3, bf16[4,3,128,128]{3,2,1,0:T(8,128)(2,1)S(1)} %all_to_all.20.refs_0_, bf16[4,2,128,128]{3,2,1,0:T(8,128)(2,1)S(1)} %collective-permute-done.refs_1_, bf16[4,2,128,128]{3,2,1,0:T(8,128)(2,1)S(1)} %collective-permute-done.3.refs_2_, ...), custom_call_target="tpu_custom_call" | custom-call | flops 2500000000 | bytes 1048576 | tf_op jit(solution)/shard_map/attention/attend_back2/pallas_call | solution.py:106
  58.8 24.7 %all-to-all-start.1 = ((f32[4,128,128]{2,1,0:T(8,128)}), f32[4,128,128]{2,1,0:T(8,128)S(1)}, u32[]{:S(2)}, u32[]{:S(2)}) async-start(f32[4,128,128]{2,1,0:T(8,128)} %attend_back2.1), calls=%async_computation.1 | async-start | bytes 524288 | tf_op jit(solution)/shard_map/attention/all_to_all | solution.py:228
  83.5 0.6 pad_bitcast_fusion.1.starts
  84.1 6.9 %all-to-all-done.1.heads = f32[4,128,128]{2,1,0:T(8,128)S(1)} async-done(((f32[4,128,128]{2,1,0:T(8,128)}), f32[4,128,128]{2,1,0:T(8,128)S(1)}, u32[]{:S(2)}, u32[]{:S(2)}) %all-to-all-start.1) | async-done | bytes 262176 | tf_op jit(solution)/shard_map/attention/all_to_all | solution.py:228
  90.9 0.0 copy-start.4
  90.9 0.7 copy-done.4
  91.6 1.8 %stream.1 = (f32[128,512]{1,0:T(8,128)}, f32[16,1,128]{2,1,0:T(1,128)}) custom-call(f32[128,512]{1,0:T(8,128)} %hyena.1.base, f32[4,128,128]{2,1,0:T(8,128)} %copy-done.4), custom_call_target="tpu_custom_call" | custom-call | tf_op jit(solution)/shard_map/mean_square/stream/pallas_call | solution.py:231
  93.4 0.0 copy-start.7
  93.4 6.9 %all-to-all-start.2 = ((f32[16,1,128]{2,1,0:T(1,128)}), f32[16,1,128]{2,1,0:T(1,128)S(1)}, u32[]{:S(2)}, u32[]{:S(2)}) async-start(f32[16,1,128]{2,1,0:T(1,128)} %get-tuple-element.31), calls=%async_computation.2 | async-start | bytes 16384 | tf_op jit(solution)/shard_map/mean_square/all_to_all | solution.py:239
  100.3 0.0 copy-done.7
  100.3 0.5 pad_bitcast_fusion.lengths
  100.8 5.7 %all-to-all-done.2.parts = f32[16,1,128]{2,1,0:T(1,128)S(1)} async-done(((f32[16,1,128]{2,1,0:T(1,128)}), f32[16,1,128]{2,1,0:T(1,128)S(1)}, u32[]{:S(2)}, u32[]{:S(2)}) %all-to-all-start.2) | async-done | bytes 8224 | tf_op jit(solution)/shard_map/mean_square/all_to_all | solution.py:239
  106.5 0.0 copy-start.5
  106.6 0.6 copy-done.5
  107.1 1.5 %records.1 = (f32[128,128]{1,0:T(8,128)}, f32[32,1,128]{2,1,0:T(1,128)}) custom-call(s32[3]{0:T(128)} %copy-done, s32[1,128]{1,0:T(1,128)} %pad_bitcast_fusion.1.starts, s32[1,128]{1,0:T(1,128)} %pad_bitcast_fusion.lengths, f32[16,1,128]{2,1,0:T(1,128)} %copy-done.5), custom_call_target="tpu_custom_call" | custom-call | tf_op jit(solution)/shard_map/record_energy/records/pallas_call | solution.py:242
  108.7 22.8 %all-to-all-start.3 = ((f32[32,1,128]{2,1,0:T(1,128)}), f32[32,1,128]{2,1,0:T(1,128)S(1)}, u32[]{:S(2)}, u32[]{:S(2)}) async-start(f32[32,1,128]{2,1,0:T(1,128)} %get-tuple-element.33), calls=%async_computation.3 | async-start | bytes 32768 | tf_op jit(solution)/shard_map/record_energy/all_to_all | solution.py:251
  131.5 1.7 %scale.1 = f32[128,512]{1,0:T(8,128)} custom-call(f32[128,512]{1,0:T(8,128)} %get-tuple-element.30.stream, f32[128,128]{1,0:T(8,128)} %get-tuple-element.32.mean, f32[1,512]{1,0:T(1,128)} %bitcast.13), custom_call_target="tpu_custom_call" | custom-call | flops 1000000000 | bytes 1048576 | tf_op jit(solution)/shard_map/scale/pallas_call | solution.py:253
  133.2 10.0 %all-to-all-done.3 = f32[32,1,128]{2,1,0:T(1,128)S(1)} async-done(((f32[32,1,128]{2,1,0:T(1,128)}), f32[32,1,128]{2,1,0:T(1,128)S(1)}, u32[]{:S(2)}, u32[]{:S(2)}) %all-to-all-start.3) | async-done | bytes 16416 | tf_op jit(solution)/shard_map/record_energy/all_to_all | solution.py:251
  143.2 0.1 reduce_sum.9
  143.3 0.5 convert_divide_fusion
  (1 shorter events, 0.0 us)
Async XLA Ops:
  16.7 24.9 %collective-permute-start.1 = (bf16[4,2,128,128]{3,2,1,0:T(8,128)(2,1)S(1)}, bf16[4,2,128,128]{3,2,1,0:T(8,128)(2,1)S(1)}, u32[]{:S(2)}, u32[]{:S(2)}) collective-permute-start(bf16[4,2,128,128]{3,2,1,0:T(8,128)(2,1)S(1)} %slice.12), channel_id=1, source_target_pairs={{0,16},{16,0},{1,17},{17,1},{2,18},{18,2},{3,19},{19,3},{4,20},{20... | collective-permute-start | bytes 786440 | tf_op jit(solution)/shard_map/keys_values_from_before/ppermute | solution.py:205
  23.6 20.3 %collective-permute-start.4 = (bf16[4,2,128,128]{3,2,1,0:T(8,128)(2,1)S(1)}, bf16[4,2,128,128]{3,2,1,0:T(8,128)(2,1)S(1)}, u32[]{:S(2)}, u32[]{:S(2)}) collective-permute-start(bf16[4,2,128,128]{3,2,1,0:T(8,128)(2,1)S(1)} %slice.12), channel_id=1, source_target_pairs={{0,128},{128,256},{256,384},{1,129},{129,257},{257,385},{2,130},{1... | collective-permute-start | bytes 786440 | tf_op jit(solution)/shard_map/keys_values_from_before/ppermute | solution.py:203
  33.1 12.9 %copy-start.2 = (s32[16]{0:T(128)S(1)}, s32[16]{0:T(128)}, u32[]{:S(2)}) copy-start(s32[16]{0:T(128)} %starts.7) | copy-start | bytes 196
  33.2 14.8 %copy-start = (s32[3]{0:T(128)}, s32[3]{0:T(128)S(1)}, u32[]{:S(2)}) copy-start(s32[3]{0:T(128)S(1)} %pad_add_fusion.scalars) | copy-start | bytes 40
  33.2 17.7 %collective-permute-start = (bf16[4,2,128,128]{3,2,1,0:T(8,128)(2,1)S(1)}, bf16[4,2,128,128]{3,2,1,0:T(8,128)(2,1)S(1)}, u32[]{:S(2)}, u32[]{:S(2)}) collective-permute-start(bf16[4,2,128,128]{3,2,1,0:T(8,128)(2,1)S(1)} %slice.12), channel_id=1, source_target_pairs={{0,256},{128,384},{1,257},{129,385},{2,258},{130,386},{3,259},{131... | collective-permute-start | bytes 786440 | tf_op jit(solution)/shard_map/keys_values_from_before/ppermute | solution.py:204
  41.6 6.3 %collective-permute-start.2 = (bf16[2,16,512]{2,1,0:T(8,128)(2,1)S(1)}, bf16[2,16,512]{2,1,0:T(8,128)(2,1)S(1)}, u32[]{:S(2)}, u32[]{:S(2)}) collective-permute-start(bf16[2,16,512]{2,1,0:T(8,128)(2,1)S(1)} %slice.13), channel_id=1, source_target_pairs={{0,16},{16,32},{32,48},{48,64},{64,80},{80,96},{96,112},{112,128},... | collective-permute-start | bytes 98312 | tf_op jit(solution)/shard_map/hyena/ppermute | solution.py:211
  43.9 9.4 %collective-permute-start.5 = (bf16[4,2,128,128]{3,2,1,0:T(8,128)(2,1)S(1)}, bf16[4,2,128,128]{3,2,1,0:T(8,128)(2,1)S(1)}, u32[]{:S(2)}, u32[]{:S(2)}) collective-permute-start(bf16[4,2,128,128]{3,2,1,0:T(8,128)(2,1)S(1)} %collective-permute-done.4.refs_1_), channel_id=1, source_target_pairs={{0,16},{16,0},{1,17},{17,1},{2,18},{18,2},{3,19},{19,3},{4,20},{20... | collective-permute-start | bytes 786440 | tf_op jit(solution)/shard_map/keys_values_from_before/ppermute | solution.py:206
  48.0 0.6 copy-start.6
  50.9 2.5 %copy-start.1 = (s32[3]{0:T(128)S(1)}, s32[3]{0:T(128)}, u32[]{:S(2)}) copy-start(s32[3]{0:T(128)} %copy-done) | copy-start | bytes 40
  50.9 2.5 %copy-start.3 = (s32[16]{0:T(128)S(1)}, s32[16]{0:T(128)}, u32[]{:S(2)}) copy-start(s32[16]{0:T(128)} %starts.7) | copy-start | bytes 196
  50.9 4.9 %collective-permute-start.3 = (bf16[4,2,128,128]{3,2,1,0:T(8,128)(2,1)S(1)}, bf16[4,2,128,128]{3,2,1,0:T(8,128)(2,1)S(1)}, u32[]{:S(2)}, u32[]{:S(2)}) collective-permute-start(bf16[4,2,128,128]{3,2,1,0:T(8,128)(2,1)S(1)} %collective-permute-done.refs_1_), channel_id=1, source_target_pairs={{0,16},{16,0},{1,17},{17,1},{2,18},{18,2},{3,19},{19,3},{4,20},{20... | collective-permute-start | bytes 786440 | tf_op jit(solution)/shard_map/attention/ppermute | solution.py:225
  58.8 32.1 %all-to-all-start.1 = ((f32[4,128,128]{2,1,0:T(8,128)}), f32[4,128,128]{2,1,0:T(8,128)S(1)}, u32[]{:S(2)}, u32[]{:S(2)}) async-start(f32[4,128,128]{2,1,0:T(8,128)} %attend_back2.1), calls=%async_computation.1 | async-start | bytes 524288 | tf_op jit(solution)/shard_map/attention/all_to_all | solution.py:228
  90.9 0.7 copy-start.4
  93.4 6.9 %copy-start.7 = (s32[16]{0:T(128)S(1)}, s32[16]{0:T(128)}, u32[]{:S(2)}) copy-start(s32[16]{0:T(128)} %param.14) | copy-start | bytes 196
  93.4 13.1 %all-to-all-start.2 = ((f32[16,1,128]{2,1,0:T(1,128)}), f32[16,1,128]{2,1,0:T(1,128)S(1)}, u32[]{:S(2)}, u32[]{:S(2)}) async-start(f32[16,1,128]{2,1,0:T(1,128)} %get-tuple-element.31), calls=%async_computation.2 | async-start | bytes 16384 | tf_op jit(solution)/shard_map/mean_square/all_to_all | solution.py:239
  106.5 0.6 copy-start.5
  108.7 34.5 %all-to-all-start.3 = ((f32[32,1,128]{2,1,0:T(1,128)}), f32[32,1,128]{2,1,0:T(1,128)S(1)}, u32[]{:S(2)}, u32[]{:S(2)}) async-start(f32[32,1,128]{2,1,0:T(1,128)} %get-tuple-element.33), calls=%async_computation.3 | async-start | bytes 32768 | tf_op jit(solution)/shard_map/record_energy/all_to_all | solution.py:251

commit v3 on v2

v3 whole, which is shorter than its diff:
```python
import functools

import jax
import jax.numpy as jnp
from jax import lax
from jax.experimental import pallas as pl
from jax.experimental.pallas import tpu as pltpu
from jax.sharding import Mesh
from jax.sharding import PartitionSpec as P

D = 8192
HEAD_DIM = 128
GROUP = 4
MASKED = -1e30
SCALE = HEAD_DIM**-0.5 * 1.4426950408889634
POSITIONS = ("z", "core")
CHIPS = 16
LONG = 2048
SMEM = pl.BlockSpec(memory_space=pltpu.SMEM)
VMEM = pl.BlockSpec(memory_space=pltpu.VMEM)


def cost(nanoseconds):
    return pl.CostEstimate(flops=nanoseconds * 1_000_000, bytes_accessed=1 << 20, transcendentals=0)


def pack_kernel(x_ref, out_ref):
    for head in range(GROUP):
        for stream in range(3):
            out_ref[head, stream] = x_ref[stream, :, head * HEAD_DIM : (head + 1) * HEAD_DIM]


def pack(streams):
    rows = streams.shape[1]
    return pl.pallas_call(
        pack_kernel,
        out_shape=jax.ShapeDtypeStruct((GROUP, 3, rows, HEAD_DIM), streams.dtype),
        name="pack_heads",
    )(streams)


def attend_rows(q, query_pos, row_start, sources, state):
    rows = q.shape[0]
    scores = []
    for keys, _, first in sources:
        s = lax.dot_general(q, keys, (((1,), (1,)), ((), ())), preferred_element_type=jnp.float32)
        key_pos = jnp.concatenate(
            [here + lax.broadcasted_iota(jnp.int32, (1, rows), 1) for here in first], axis=1
        )
        allowed = (key_pos >= row_start) & (key_pos <= query_pos)
        scores.append(jnp.where(allowed, s * SCALE, MASKED))
    top = functools.reduce(jnp.maximum, [jnp.max(s, axis=1, keepdims=True) for s in scores])
    if state is not None:
        top = jnp.maximum(top, state[0])
    total = jnp.zeros((rows, 1), jnp.float32)
    summed = jnp.zeros((rows, HEAD_DIM), jnp.float32)
    for s, (_, values, _) in zip(scores, sources):
        weights = jnp.exp2(s - top)
        total = total + jnp.sum(weights, axis=1, keepdims=True)
        summed = summed + jnp.dot(
            weights.astype(jnp.bfloat16), values, preferred_element_type=jnp.float32
        )
    if state is not None:
        factor = jnp.exp2(state[0] - top)
        total = total + state[1] * factor
        summed = summed + state[2] * factor
    return top, total, summed


def chip_position(cut, group, place, core, rows):
    chip = lax.rem(group * GROUP + place + (cut + 2 * CHIPS), CHIPS)
    return (chip * 2 + core) * rows


def blocks_of(ref, low, high, offset=0):
    rows = ref.shape[2]
    return [ref[low:high, offset + i].reshape((high - low) * rows, HEAD_DIM) for i in range(2)]


def attend_kernel(cut, phase, scalars, starts, q_ref, *refs):
    group, core = scalars[0], scalars[1]
    rows = q_ref.shape[2]
    place = lax.broadcasted_iota(jnp.int32, (rows, 1), 0)

    def positions(of_group, block, of_core):
        return chip_position(cut, of_group, block, of_core, rows)

    for block in range(GROUP):
        q = q_ref[block, 0]
        query_pos = positions(group, block, core) + place
        row_start = row_starts(starts, query_pos)
        if phase == 0:
            other_ref = refs[0]
            outs = refs[2:5]
            state = None
            sources = [
                (
                    *blocks_of(q_ref, 0, block + 1, 1),
                    [positions(group, i, core) for i in range(block + 1)],
                ),
                (
                    *blocks_of(other_ref, 0, block + 1),
                    [positions(group, i, 1 - core) for i in range(block + 1)],
                ),
            ]
        else:
            key_core = core if phase == 1 else 1 - core
            state = [ref[block] for ref in refs[1:4]]
            sources = [
                (
                    *blocks_of(refs[0], 0, GROUP),
                    [positions(group - 1, i, key_core) for i in range(GROUP)],
                )
            ]
        top, total, summed = attend_rows(q, query_pos, row_start, sources, state)
        if phase < 2:
            outs = refs[2:5] if phase == 0 else refs[4:7]
            outs[0][block], outs[1][block], outs[2][block] = top, total, summed
        else:
            back_ref, out_ref = refs[4:]
            if block == 0:
                far_top = jnp.broadcast_to(back_ref[rows : rows + 1], (rows, rows)).T[:, :1]
                joint = jnp.maximum(top, far_top)
                near, far = jnp.exp2(top - joint), jnp.exp2(far_top - joint)
                total = total * near + far
                summed = summed * near + back_ref[:rows] * far
            out_ref[block] = summed / total
    if phase == 0:
        other_ref, far_ref = refs[:2]
        away_ref = refs[5]
        query_pos = positions(group + 2, 0, core) + place
        sources = [
            (*blocks_of(q_ref, 0, GROUP, 1), [positions(group, i, core) for i in range(GROUP)]),
            (*blocks_of(other_ref, 0, GROUP), [positions(group, i, 1 - core) for i in range(GROUP)]),
        ]
        top, total, summed = attend_rows(
            far_ref[...], query_pos, row_starts(starts, query_pos), sources, None
        )
        away_ref[:rows] = summed / total
        column = jnp.broadcast_to(top + jnp.log2(total), (rows, rows))
        away_ref[rows:] = column.T[: away_ref.shape[0] - rows]


def attend(cut, phase, scalars, starts, received, *others):
    rows = received.shape[2]
    column = jax.ShapeDtypeStruct((GROUP, rows, 1), jnp.float32)
    full = jax.ShapeDtypeStruct((GROUP, rows, HEAD_DIM), jnp.float32)
    away = jax.ShapeDtypeStruct((rows + 8, HEAD_DIM), jnp.float32)
    out_shape = ((column, column, full, away), (column, column, full), full)[phase]
    return pl.pallas_call(
        functools.partial(attend_kernel, cut, phase),
        out_shape=out_shape,
        in_specs=[SMEM, SMEM] + [VMEM] * (1 + len(others)),
        compiler_params=pltpu.CompilerParams(vmem_limit_bytes=32 * 1024 * 1024),
        cost_estimate=cost(2000),
        name=f"attend{phase}",
    )(scalars, starts, received, *others)


def row_starts(starts, positions):
    found = jnp.zeros_like(positions)
    for record in range(starts.shape[0]):
        here = starts[record]
        found = jnp.where(positions >= here, here, found)
    return found


def hyena_kernel(scalars, starts, residual, streams, rim, taps_ref, out_ref, padded):
    rows = residual.shape[0]
    edge = rim.shape[1]
    taps = taps_ref.shape[0]
    positions = scalars[2] * rows + lax.broadcasted_iota(jnp.int32, (rows, 1), 0)
    first = row_starts(starts, positions)
    padded[:edge] = rim[0].astype(jnp.float32) * rim[1].astype(jnp.float32)
    padded[edge:] = streams[1].astype(jnp.float32) * streams[2].astype(jnp.float32)
    filtered = jnp.zeros(out_ref.shape, jnp.float32)
    for tap in range(taps):
        term = taps_ref[tap : tap + 1, :] * padded[edge - tap : edge - tap + rows]
        filtered = filtered + jnp.where(positions - tap >= first, term, 0.0)
    out_ref[...] = residual[...].astype(jnp.float32) + streams[0].astype(jnp.float32) * filtered


def stream_kernel(base, heads, stream_ref, squares_ref):
    rows = base.shape[0]
    squares = jnp.zeros((rows, HEAD_DIM), jnp.float32)
    for head in range(GROUP):
        columns = slice(head * HEAD_DIM, (head + 1) * HEAD_DIM)
        value = base[:, columns] + heads[head]
        stream_ref[:, columns] = value
        squares = squares + value * value
    line = jnp.sum(squares.T, axis=0, keepdims=True)
    for device in range(squares_ref.shape[0]):
        squares_ref[device] = line


def records_kernel(scalars, starts, lengths, parts, mean_ref, sums_ref):
    rows = parts.shape[2]
    line = jnp.sum(parts[:, 0, :], axis=0, keepdims=True) / D
    mean = jnp.broadcast_to(line, (rows, rows)).T
    mean_ref[...] = mean
    position = scalars[2] * rows + lax.broadcasted_iota(jnp.int32, (rows, rows), 0)
    first = starts[...]
    inside = (position >= first) & (position < first + lengths[...])
    sums = jnp.sum(jnp.where(inside, mean, 0.0), axis=0, keepdims=True)
    for device in range(sums_ref.shape[0]):
        sums_ref[device] = sums


def scale_kernel(stream, mean, gain, out_ref):
    factor = lax.rsqrt(mean[...] + 1e-05)
    for head in range(GROUP):
        columns = slice(head * HEAD_DIM, (head + 1) * HEAD_DIM)
        out_ref[:, columns] = stream[:, columns] * factor * gain[:, columns]


def mixers(cut, packed, residual, streams, taps, starts):
    rows, width = residual.shape
    seq = lax.axis_size(POSITIONS)
    chip, core = lax.axis_index("z"), lax.axis_index("core")
    group = lax.rem(chip + CHIPS - cut, CHIPS) // GROUP
    scalars = jnp.stack([group, core, lax.axis_index(POSITIONS)]).astype(jnp.int32)
    groups = [
        [(cut + GROUP * k + i) % CHIPS for i in range(GROUP)] for k in range(CHIPS // GROUP)
    ]
    swap = [(0, 1), (1, 0)]

    def along(value, chips):
        return lax.ppermute(value, "z", [(i, (i + chips) % CHIPS) for i in range(CHIPS)])

    received = lax.all_to_all(packed, "z", 0, 0, axis_index_groups=groups, tiled=True)
    far = along(received[0, 0], -2 * GROUP)
    key_value = received[:, 1:]
    before = along(key_value, GROUP)
    other = lax.ppermute(key_value, "core", swap)
    rim = lax.ppermute(streams[1:, rows - 16 :], POSITIONS, [(i, i + 1) for i in range(seq - 1)])
    base = pl.pallas_call(
        hyena_kernel,
        out_shape=jax.ShapeDtypeStruct((rows, width), jnp.float32),
        in_specs=[SMEM, SMEM, VMEM, VMEM, VMEM, VMEM],
        out_specs=VMEM,
        scratch_shapes=[pltpu.VMEM((rows + 16, width), jnp.float32)],
        cost_estimate=cost(2000),
        name="hyena",
    )(scalars, starts, residual, streams, rim, taps)
    *state, away = attend(cut, 0, scalars, starts, received, other, far)
    back = along(away, 2 * GROUP)
    before, base, state = lax.optimization_barrier((before, base, state))
    before_other = lax.ppermute(before, "core", swap)
    state = attend(cut, 1, scalars, starts, received, before, *state)
    out = attend(cut, 2, scalars, starts, received, before_other, *state, back)
    heads = lax.all_to_all(out, "z", 0, 0, axis_index_groups=groups, tiled=True)
    return base, heads


def on_device(
    residual,
    hyena_streams,
    hyena_filter,
    attention_streams,
    norm_gain,
    record_starts,
    record_lengths,
    segment_ids,
):
    rows, width = residual.shape
    records = record_starts.shape[0]
    seq, mp = lax.axis_size(POSITIONS), lax.axis_size("mp")
    place = lax.axis_index(POSITIONS)

    packed = pack(attention_streams.transpose(1, 0, 2))
    long_start = jnp.sum(jnp.where(record_lengths == LONG, record_starts, 0))
    base, heads = lax.switch(
        lax.rem(long_start // (2 * rows), GROUP),
        [functools.partial(mixers, cut) for cut in range(GROUP)],
        packed,
        residual,
        hyena_streams.transpose(1, 0, 2),
        hyena_filter,
        record_starts,
    )
    scalars = jnp.stack([place, place, place]).astype(jnp.int32)

    with jax.named_scope("mean_square"):
        stream, squares = pl.pallas_call(
            stream_kernel,
            out_shape=(
                jax.ShapeDtypeStruct((rows, width), jnp.float32),
                jax.ShapeDtypeStruct((mp, 1, rows), jnp.float32),
            ),
            name="stream",
        )(base, heads)
        parts = lax.all_to_all(squares, "mp", 0, 0, tiled=True)
    with jax.named_scope("record_energy"):
        lines = [jnp.pad(x, (0, 128 - records))[None, :] for x in (record_starts, record_lengths)]
        mean, sums = pl.pallas_call(
            records_kernel,
            out_shape=(
                jax.ShapeDtypeStruct((rows, rows), jnp.float32),
                jax.ShapeDtypeStruct((seq, 1, 128), jnp.float32),
            ),
            in_specs=[SMEM, VMEM, VMEM, VMEM],
            name="records",
        )(scalars, *lines, parts)
        sums = lax.all_to_all(sums, POSITIONS, 0, 0, tiled=True)
        record_energy = jnp.sum(sums, axis=(0, 1))[:records] / record_lengths.astype(jnp.float32)
    mixed = pl.pallas_call(
        scale_kernel,
        out_shape=jax.ShapeDtypeStruct((rows, width), jnp.float32),
        cost_estimate=cost(1000),
        name="scale",
    )(stream, mean, norm_gain[None, :])
    return (mixed, record_energy)


def solution(mesh):
    fine = Mesh(mesh.devices.reshape(CHIPS, 2, mesh.shape["mp"]), ("z", "core", "mp"))
    return jax.shard_map(
        on_device,
        mesh=fine,
        in_specs=(
            P(POSITIONS, "mp"),
            P(POSITIONS, None, "mp"),
            P(None, "mp"),
            P(POSITIONS, None, "mp"),
            P("mp"),
            P(),
            P(),
            P(POSITIONS),
        ),
        out_specs=(P(POSITIONS, "mp"), P()),
        check_vma=False,
    )
```

time: 144 us -> 142 us (0.986)
  starting transfers between devices: 85.2 us -> 58.2 us
  waiting for transfers between devices: 22.6 us -> 47.1 us
  Pallas kernels: 16.6 us -> 14 us
  between operations: 0.82 us -> 3.3 us
  other arithmetic: 0.65 us -> 2.53 us
    ppermute x6, waiting for transfers between devices: 0.02 us -> 25.2 us  [the longest x3 25.2 us: along(): lax.ppermute(value, 'z', [(i, (i + chips) % CHIPS) for i in range(CHIPS)])]
    all_to_all x1, starting transfers between devices: 22.8 us -> 11.3 us  [on_device(): sums = lax.all_to_all(sums, POSITIONS, 0, 0, tiled=True)]
    all_to_all x1, starting transfers between devices: 24.7 us -> 14.4 us  [mixers(): lax.all_to_all(packed, 'z', 0, 0, axis_index_groups=groups, tiled=True)]
    ppermute x6, starting transfers between devices: 30.8 us -> 25.6 us  [the longest x3 17.1 us: along(): lax.ppermute(value, 'z', [(i, (i + chips) % CHIPS) for i in range(CHIPS)])]
    pallas_call x4, Pallas kernels: 9.69 us -> 8.11 us  [the longest x3 6.75 us: attend(): pl.pallas_call(functools.partial(attend_kernel, cut, phase), out_shape=ou...]
  transfers between devices with their start and end apart: 9 -> 9, of which waited for: 3 -> 5; matrix products, arithmetic and copies ran while one was open for 1% -> 1% of each run, Pallas kernels for 6% -> 5%
where the time goes in v3:
time: 142 us
  starting transfers between devices  58.2 us (41%)
  waiting for transfers between devices  47.1 us (33%)
  Pallas kernels  14 us (10%)
  blocking collectives  13.8 us (10%)
  between operations  3.3 us (2%)
  other arithmetic  2.53 us (2%)
  local copies, waits for them, and re-layouts  2.48 us (2%)
    ppermute x3, waiting for transfers between devices, along(): lax.ppermute(value, 'z', [(i, (i + chips) % CHIPS) for i in range(CHIPS)])  25.2 us
    ppermute x3, starting transfers between devices, along(): lax.ppermute(value, 'z', [(i, (i + chips) % CHIPS) for i in range(CHIPS)])  17.1 us
    all_to_all x1, starting transfers between devices, mixers(): lax.all_to_all(packed, 'z', 0, 0, axis_index_groups=groups, tiled=True)  14.4 us
    all_to_all x1, blocking collectives, mixers(): heads = lax.all_to_all(out, 'z', 0, 0, axis_index_groups=groups, tiled=True)  13.8 us
    all_to_all x1, starting transfers between devices, on_device(): sums = lax.all_to_all(sums, POSITIONS, 0, 0, tiled=True)  11.3 us
    all_to_all x1, waiting for transfers between devices, on_device(): sums = lax.all_to_all(sums, POSITIONS, 0, 0, tiled=True)  10 us
    all_to_all x1, starting transfers between devices, on_device(): parts = lax.all_to_all(squares, 'mp', 0, 0, tiled=True)  6.88 us
    pallas_call x3, Pallas kernels, attend(): pl.pallas_call(functools.partial(attend_kernel, cut, phase), out_shape=ou...  6.75 us
  transfers between devices with their start and end apart: 9, of which 5 were waited for; matrix products, arithmetic and copies ran while one was open for 1% of the time, Pallas kernels for 5%

profile of v3, /device:TPU:1, one launch (start us, length us, event | category | flops | bytes accessed | tf_op | source)
XLA Modules:
  0.0 141.6 jit_solution(11886916384528829738)
XLA Ops:
  0.6 1.3 fusion
  4.6 0.0 copy-start.4
  4.6 0.0 copy-start.8
  4.6 0.0 copy-start.13
  4.6 1.9 %pack_heads.1 = bf16[4,3,128,128]{3,2,1,0:T(8,128)(2,1)} custom-call(bf16[3,128,512]{2,1,0:T(8,128)(2,1)} %bitcast.27), custom_call_target="tpu_custom_call" | custom-call | tf_op jit(solution)/shard_map/pack_heads/pallas_call | solution.py:35
  6.5 0.0 copy-start.6
  6.5 0.0 copy-done.4
  6.5 0.0 copy-done.8
  6.5 0.0 copy-done.13
  6.5 0.6 copy-done.6
  7.1 94.6 %conditional.1 = (f32[128,512]{1,0:T(8,128)S(1)}, f32[4,128,128]{2,1,0:T(8,128)S(1)}) conditional(s32[]{:T(128)} %clamp.3, (bf16[4,3,128,128]{3,2,1,0:T(8,128)(2,1)}, bf16[3,128,512]{2,1,0:T(8,128)(2,1)S(1)}, s32[16]{0:T(128)S(1)}, bf16[128,512]{1,0:T(8,128)(2,1)S(1)}, f32[7,512]{1,0:T(8,128)S(1)}) %tuple.47, ...), branch_computations={%region_1.2_spmd, %region_2.3_spmd, %region_3.4_spmd, %region_4.5_... | conditional | flops 8000000000 | bytes 10371801 | solution.py:272
  7.1 14.4 %all-to-all-start.2 = ((bf16[4,3,128,128]{3,2,1,0:T(8,128)(2,1)}), bf16[4,3,128,128]{3,2,1,0:T(8,128)(2,1)S(1)}, u32[]{:S(2)}, u32[]{:S(2)}) async-start(bf16[4,3,128,128]{3,2,1,0:T(8,128)(2,1)} %get-tuple-element.57), calls=%async_computation.2 | async-start | bytes 786432 | tf_op jit(solution)/shard_map/cond/branch_1_fun/all_to_all | solution.py:230
  21.5 1.9 %collective-permute-start.7 = (bf16[2,16,512]{2,1,0:T(8,128)(2,1)S(1)}, bf16[2,16,512]{2,1,0:T(8,128)(2,1)S(1)}, u32[]{:S(2)}, u32[]{:S(2)}) collective-permute-start(bf16[2,16,512]{2,1,0:T(8,128)(2,1)S(1)} %slice.30), channel_id=1, source_target_pairs={{0,16},{16,32},{32,48},{48,64},{64,80},{80,96},{96,112},{112,128},... | collective-permute-start | bytes 98312 | tf_op jit(solution)/shard_map/cond/branch_1_fun/ppermute | solution.py:235
  23.4 0.7 pad_add_fusion.1.scalars
  24.1 6.2 %all-to-all-done.2.q_ref = bf16[4,3,128,128]{3,2,1,0:T(8,128)(2,1)S(1)} async-done(((bf16[4,3,128,128]{3,2,1,0:T(8,128)(2,1)}), bf16[4,3,128,128]{3,2,1,0:T(8,128)(2,1)S(1)}, u32[]{:S(2)}, u32[]{:S(2)}) %all-to-all-start.2) | async-done | bytes 393248 | tf_op jit(solution)/shard_map/cond/branch_1_fun/all_to_all | solution.py:230
  30.3 4.0 %collective-permute-start.8 = (bf16[4,2,128,128]{3,2,1,0:T(8,128)(2,1)S(1)}, bf16[4,2,128,128]{3,2,1,0:T(8,128)(2,1)S(1)}, u32[]{:S(2)}, u32[]{:S(2)}) collective-permute-start(bf16[4,2,128,128]{3,2,1,0:T(8,128)(2,1)S(1)} %slice.42), channel_id=1, source_target_pairs={{0,16},{16,0},{1,17},{17,1},{2,18},{18,2},{3,19},{19,3},{4,20},{20... | collective-permute-start | bytes 786440 | tf_op jit(solution)/shard_map/cond/branch_1_fun/ppermute | solution.py:234
  34.3 1.9 %collective-permute-start.6 = (bf16[4,2,128,128]{3,2,1,0:T(8,128)(2,1)S(1)}, bf16[4,2,128,128]{3,2,1,0:T(8,128)(2,1)S(1)}, u32[]{:S(2)}, u32[]{:S(2)}) collective-permute-start(bf16[4,2,128,128]{3,2,1,0:T(8,128)(2,1)S(1)} %slice.42), channel_id=1, source_target_pairs={{0,128},{32,160},{64,192},{96,224},{128,256},{160,288},{192,320},{... | collective-permute-start | bytes 786440 | tf_op jit(solution)/shard_map/cond/branch_1_fun/ppermute | solution.py:228
  36.3 10.3 %collective-permute-start.9 = (bf16[128,128]{1,0:T(8,128)(2,1)S(1)}, bf16[128,128]{1,0:T(8,128)(2,1)S(1)}, u32[]{:S(2)}, u32[]{:S(2)}) collective-permute-start(bf16[128,128]{1,0:T(8,128)(2,1)S(1)} %slice_bitcast_fusion.1), channel_id=1, source_target_pairs={{0,256},{32,288},{64,320},{96,352},{128,384},{160,416},{192,448},{... | collective-permute-start | bytes 98312 | tf_op jit(solution)/shard_map/cond/branch_1_fun/ppermute | solution.py:228
  46.5 0.0 collective-permute-done.7.rim
  46.5 0.0 copy-start.12
  46.5 0.6 copy-done.12
  47.2 0.0 copy-start.1
  47.2 1.4 hyena.5
  48.5 17.9 %collective-permute-done.9.refs_1_ = bf16[128,128]{1,0:T(8,128)(2,1)S(1)} collective-permute-done((bf16[128,128]{1,0:T(8,128)(2,1)S(1)}, bf16[128,128]{1,0:T(8,128)(2,1)S(1)}, u32[]{:S(2)}, u32[]{:S(2)}) %collective-permute-start.9) | collective-permute-done | bytes 32800 | tf_op jit(solution)/shard_map/cond/branch_1_fun/ppermute | solution.py:228
  66.4 0.0 collective-permute-done.8.refs_0_
  66.4 0.0 copy-done.1
  66.4 2.4 %attend0.5 = (f32[4,128,1]{2,1,0:T(8,128)S(1)}, f32[4,128,1]{2,1,0:T(8,128)S(1)}, f32[4,128,128]{2,1,0:T(8,128)S(1)}, f32[136,128]{1,0:T(8,128)S(1)}) custom-call(s32[3]{0:T(128)S(1)} %copy-done.1, s32[16]{0:T(128)S(1)} %get-tuple-element.58.starts, bf16[4,3,128,128]{3,2,1,0:T(8,128)(2,1)S(1)} %all-to-all-done.2.q_ref, ...), custom_call_target="tpu_custom_call" | custom-call | flops 2000000000 | bytes 1048576 | tf_op jit(solution)/shard_map/cond/branch_1_fun/attend0/pallas_call | solution.py:150
  68.8 0.0 collective-permute-done.6.refs_0_
  68.8 2.5 %collective-permute-start.10 = (bf16[4,2,128,128]{3,2,1,0:T(8,128)(2,1)S(1)}, bf16[4,2,128,128]{3,2,1,0:T(8,128)(2,1)S(1)}, u32[]{:S(2)}, u32[]{:S(2)}) collective-permute-start(bf16[4,2,128,128]{3,2,1,0:T(8,128)(2,1)S(1)} %collective-permute-done.6.refs_0_), channel_id=1, source_target_pairs={{0,16},{16,0},{1,17},{17,1},{2,18},{18,2},{3,19},{19,3},{4,20},{20... | collective-permute-start | bytes 786440 | tf_op jit(solution)/shard_map/cond/branch_1_fun/ppermute | solution.py:248
  71.3 4.9 %collective-permute-start.11 = (f32[136,128]{1,0:T(8,128)S(1)}, f32[136,128]{1,0:T(8,128)S(1)}, u32[]{:S(2)}, u32[]{:S(2)}) collective-permute-start(f32[136,128]{1,0:T(8,128)S(1)} %get-tuple-element.73), channel_id=1, source_target_pairs={{0,256},{32,288},{64,320},{96,352},{128,384},{160,416},{192,448},{... | collective-permute-start | bytes 208904 | tf_op jit(solution)/shard_map/cond/branch_1_fun/ppermute | solution.py:228
  76.3 2.1 %attend1.5 = (f32[4,128,1]{2,1,0:T(8,128)S(1)}, f32[4,128,1]{2,1,0:T(8,128)S(1)}, f32[4,128,128]{2,1,0:T(8,128)S(1)}) custom-call(s32[3]{0:T(128)S(1)} %copy-done.1, s32[16]{0:T(128)S(1)} %get-tuple-element.58.starts, bf16[4,3,128,128]{3,2,1,0:T(8,128)(2,1)S(1)} %all-to-all-done.2.q_ref, bf16[4,2,128,128]{3,2,1,0:T(8,128)(2,1)S(1)} %collective-permute-done.6.refs_0_, ...), custom_call_target="tpu_custom_call" | custom-call | flops 2000000000 | bytes 1048576 | tf_op jit(solution)/shard_map/cond/branch_1_fun/attend1/pallas_call | solution.py:150
  78.4 7.3 %collective-permute-done.11.refs_4_ = f32[136,128]{1,0:T(8,128)S(1)} collective-permute-done((f32[136,128]{1,0:T(8,128)S(1)}, f32[136,128]{1,0:T(8,128)S(1)}, u32[]{:S(2)}, u32[]{:S(2)}) %collective-permute-start.11) | collective-permute-done | bytes 69664 | tf_op jit(solution)/shard_map/cond/branch_1_fun/ppermute | solution.py:228
  85.7 0.0 collective-permute-done.10.refs_0_
  85.7 2.2 %attend2.5 = f32[4,128,128]{2,1,0:T(8,128)S(1)} custom-call(s32[3]{0:T(128)S(1)} %copy-done.1, s32[16]{0:T(128)S(1)} %get-tuple-element.58.starts, bf16[4,3,128,128]{3,2,1,0:T(8,128)(2,1)S(1)} %all-to-all-done.2.q_ref, bf16[4,2,128,128]{3,2,1,0:T(8,128)(2,1)S(1)} %collective-permute-done.10.refs_0_, f32[4,128,1]{2,1,0:T(8,128)S(1)} %get-tuple-element.70.refs_1_, ...), custom_call_target="tpu_custom_call" | custom-call | flops 2000000000 | bytes 1048576 | tf_op jit(solution)/shard_map/cond/branch_1_fun/attend2/pallas_call | solution.py:150
  88.0 13.8 %all_to_all.43 = f32[4,128,128]{2,1,0:T(8,128)S(1)} all-to-all(f32[4,128,128]{2,1,0:T(8,128)S(1)} %attend2.5), channel_id=1, replica_groups={{32,64,96,128},{160,192,224,256},{288,320,352,384},{416,448,480,0},{33,..., dimensions={0} | all-to-all | bytes 524288 | tf_op jit(solution)/shard_map/cond/branch_1_fun/all_to_all | solution.py:251
  101.7 0.7 stream.1
  102.5 0.0 copy-start.7
  102.5 6.9 %all-to-all-start.8 = ((f32[16,1,128]{2,1,0:T(1,128)}), f32[16,1,128]{2,1,0:T(1,128)S(1)}, u32[]{:S(2)}, u32[]{:S(2)}) async-start(f32[16,1,128]{2,1,0:T(1,128)} %get-tuple-element.119), calls=%async_computation.8 | async-start | bytes 16384 | tf_op jit(solution)/shard_map/mean_square/all_to_all | solution.py:292
  109.4 0.0 copy-done.7
  109.4 0.6 pad_bitcast_fusion
  110.0 5.7 %all-to-all-done.8.parts = f32[16,1,128]{2,1,0:T(1,128)S(1)} async-done(((f32[16,1,128]{2,1,0:T(1,128)}), f32[16,1,128]{2,1,0:T(1,128)S(1)}, u32[]{:S(2)}, u32[]{:S(2)}) %all-to-all-start.8) | async-done | bytes 8224 | tf_op jit(solution)/shard_map/mean_square/all_to_all | solution.py:292
  115.7 0.0 copy-start.5
  115.7 0.5 stack.54.scalars
  116.2 0.1 copy-done.5
  116.3 1.5 %records.1 = (f32[128,128]{1,0:T(8,128)}, f32[32,1,128]{2,1,0:T(1,128)}) custom-call(s32[3]{0:T(128)} %stack.54.scalars, s32[1,128]{1,0:T(1,128)} %get-tuple-element.123.starts, s32[1,128]{1,0:T(1,128)} %get-tuple-element.122.lengths, f32[16,1,128]{2,1,0:T(1,128)} %copy-done.5), custom_call_target="tpu_custom_call" | custom-call | tf_op jit(solution)/shard_map/record_energy/records/pallas_call | solution.py:295
  117.9 11.3 %all-to-all-start.9 = ((f32[32,1,128]{2,1,0:T(1,128)}), f32[32,1,128]{2,1,0:T(1,128)S(1)}, u32[]{:S(2)}, u32[]{:S(2)}) async-start(f32[32,1,128]{2,1,0:T(1,128)} %get-tuple-element.121), calls=%async_computation.9 | async-start | bytes 32768 | tf_op jit(solution)/shard_map/record_energy/all_to_all | solution.py:304
  129.2 1.7 %scale.1 = f32[128,512]{1,0:T(8,128)} custom-call(f32[128,512]{1,0:T(8,128)} %get-tuple-element.118.stream, f32[128,128]{1,0:T(8,128)} %get-tuple-element.120.mean, f32[1,512]{1,0:T(1,128)} %bitcast.32), custom_call_target="tpu_custom_call" | custom-call | flops 1000000000 | bytes 1048576 | tf_op jit(solution)/shard_map/scale/pallas_call | solution.py:306
  130.9 10.0 %all-to-all-done.9 = f32[32,1,128]{2,1,0:T(1,128)S(1)} async-done(((f32[32,1,128]{2,1,0:T(1,128)}), f32[32,1,128]{2,1,0:T(1,128)S(1)}, u32[]{:S(2)}, u32[]{:S(2)}) %all-to-all-start.9) | async-done | bytes 16416 | tf_op jit(solution)/shard_map/record_energy/all_to_all | solution.py:304
  141.0 0.1 reduce_sum.19
  141.0 0.5 convert_divide_fusion
  (3 shorter events, 0.0 us)
Async XLA Ops:
  4.6 1.9 %copy-start.4 = (bf16[128,3,512]{2,0,1:T(8,128)(2,1)S(1)}, bf16[128,3,512]{2,0,1:T(8,128)(2,1)}, u32[]{:S(2)}) copy-start(bf16[128,3,512]{2,0,1:T(8,128)(2,1)} %param.13) | copy-start | bytes 1179652
  4.6 1.9 %copy-start.8 = (bf16[128,512]{1,0:T(8,128)(2,1)S(1)}, bf16[128,512]{1,0:T(8,128)(2,1)}, u32[]{:S(2)}) copy-start(bf16[128,512]{1,0:T(8,128)(2,1)} %param.12) | copy-start | bytes 393220
  4.6 1.9 %copy-start.13 = (f32[7,512]{1,0:T(8,128)S(1)}, f32[7,512]{1,0:T(8,128)}, u32[]{:S(2)}) copy-start(f32[7,512]{1,0:T(8,128)} %param.14) | copy-start | bytes 43012
  6.5 0.7 copy-start.6
  7.1 23.1 %all-to-all-start.2 = ((bf16[4,3,128,128]{3,2,1,0:T(8,128)(2,1)}), bf16[4,3,128,128]{3,2,1,0:T(8,128)(2,1)S(1)}, u32[]{:S(2)}, u32[]{:S(2)}) async-start(bf16[4,3,128,128]{3,2,1,0:T(8,128)(2,1)} %get-tuple-element.57), calls=%async_computation.2 | async-start | bytes 786432 | tf_op jit(solution)/shard_map/cond/branch_1_fun/all_to_all | solution.py:230
  21.5 25.0 %collective-permute-start.7 = (bf16[2,16,512]{2,1,0:T(8,128)(2,1)S(1)}, bf16[2,16,512]{2,1,0:T(8,128)(2,1)S(1)}, u32[]{:S(2)}, u32[]{:S(2)}) collective-permute-start(bf16[2,16,512]{2,1,0:T(8,128)(2,1)S(1)} %slice.30), channel_id=1, source_target_pairs={{0,16},{16,32},{32,48},{48,64},{64,80},{80,96},{96,112},{112,128},... | collective-permute-start | bytes 98312 | tf_op jit(solution)/shard_map/cond/branch_1_fun/ppermute | solution.py:235
  30.3 36.1 %collective-permute-start.8 = (bf16[4,2,128,128]{3,2,1,0:T(8,128)(2,1)S(1)}, bf16[4,2,128,128]{3,2,1,0:T(8,128)(2,1)S(1)}, u32[]{:S(2)}, u32[]{:S(2)}) collective-permute-start(bf16[4,2,128,128]{3,2,1,0:T(8,128)(2,1)S(1)} %slice.42), channel_id=1, source_target_pairs={{0,16},{16,0},{1,17},{17,1},{2,18},{18,2},{3,19},{19,3},{4,20},{20... | collective-permute-start | bytes 786440 | tf_op jit(solution)/shard_map/cond/branch_1_fun/ppermute | solution.py:234
  34.3 34.5 %collective-permute-start.6 = (bf16[4,2,128,128]{3,2,1,0:T(8,128)(2,1)S(1)}, bf16[4,2,128,128]{3,2,1,0:T(8,128)(2,1)S(1)}, u32[]{:S(2)}, u32[]{:S(2)}) collective-permute-start(bf16[4,2,128,128]{3,2,1,0:T(8,128)(2,1)S(1)} %slice.42), channel_id=1, source_target_pairs={{0,128},{32,160},{64,192},{96,224},{128,256},{160,288},{192,320},{... | collective-permute-start | bytes 786440 | tf_op jit(solution)/shard_map/cond/branch_1_fun/ppermute | solution.py:228
  36.3 30.1 %collective-permute-start.9 = (bf16[128,128]{1,0:T(8,128)(2,1)S(1)}, bf16[128,128]{1,0:T(8,128)(2,1)S(1)}, u32[]{:S(2)}, u32[]{:S(2)}) collective-permute-start(bf16[128,128]{1,0:T(8,128)(2,1)S(1)} %slice_bitcast_fusion.1), channel_id=1, source_target_pairs={{0,256},{32,288},{64,320},{96,352},{128,384},{160,416},{192,448},{... | collective-permute-start | bytes 98312 | tf_op jit(solution)/shard_map/cond/branch_1_fun/ppermute | solution.py:228
  46.5 0.6 copy-start.12
  47.2 19.2 %copy-start.1 = (s32[3]{0:T(128)S(1)}, s32[3]{0:T(128)}, u32[]{:S(2)}) copy-start(s32[3]{0:T(128)} %pad_add_fusion.1.scalars) | copy-start | bytes 40 | tf_op jit(solution)/shard_map/cond
  68.8 17.0 %collective-permute-start.10 = (bf16[4,2,128,128]{3,2,1,0:T(8,128)(2,1)S(1)}, bf16[4,2,128,128]{3,2,1,0:T(8,128)(2,1)S(1)}, u32[]{:S(2)}, u32[]{:S(2)}) collective-permute-start(bf16[4,2,128,128]{3,2,1,0:T(8,128)(2,1)S(1)} %collective-permute-done.6.refs_0_), channel_id=1, source_target_pairs={{0,16},{16,0},{1,17},{17,1},{2,18},{18,2},{3,19},{19,3},{4,20},{20... | collective-permute-start | bytes 786440 | tf_op jit(solution)/shard_map/cond/branch_1_fun/ppermute | solution.py:248
  71.3 14.4 %collective-permute-start.11 = (f32[136,128]{1,0:T(8,128)S(1)}, f32[136,128]{1,0:T(8,128)S(1)}, u32[]{:S(2)}, u32[]{:S(2)}) collective-permute-start(f32[136,128]{1,0:T(8,128)S(1)} %get-tuple-element.73), channel_id=1, source_target_pairs={{0,256},{32,288},{64,320},{96,352},{128,384},{160,416},{192,448},{... | collective-permute-start | bytes 208904 | tf_op jit(solution)/shard_map/cond/branch_1_fun/ppermute | solution.py:228
  102.5 6.9 %copy-start.7 = (s32[16]{0:T(128)S(1)}, s32[16]{0:T(128)}, u32[]{:S(2)}) copy-start(s32[16]{0:T(128)} %param.18) | copy-start | bytes 196
  102.5 13.2 %all-to-all-start.8 = ((f32[16,1,128]{2,1,0:T(1,128)}), f32[16,1,128]{2,1,0:T(1,128)S(1)}, u32[]{:S(2)}, u32[]{:S(2)}) async-start(f32[16,1,128]{2,1,0:T(1,128)} %get-tuple-element.119), calls=%async_computation.8 | async-start | bytes 16384 | tf_op jit(solution)/shard_map/mean_square/all_to_all | solution.py:292
  115.7 0.6 copy-start.5
  117.9 23.1 %all-to-all-start.9 = ((f32[32,1,128]{2,1,0:T(1,128)}), f32[32,1,128]{2,1,0:T(1,128)S(1)}, u32[]{:S(2)}, u32[]{:S(2)}) async-start(f32[32,1,128]{2,1,0:T(1,128)} %get-tuple-element.121), calls=%async_computation.9 | async-start | bytes 32768 | tf_op jit(solution)/shard_map/record_energy/all_to_all | solution.py:304

commit v4 on v3

v4 whole, which is shorter than its diff:
```python
import functools

import jax
import jax.numpy as jnp
from jax import lax
from jax.experimental import pallas as pl
from jax.experimental.pallas import tpu as pltpu
from jax.sharding import Mesh
from jax.sharding import PartitionSpec as P

D = 8192
HEAD_DIM = 128
GROUP = 4
MASKED = -1e30
SCALE = HEAD_DIM**-0.5 * 1.4426950408889634
POSITIONS = ("z", "core")
CHIPS = 16
LONG = 2048
SMEM = pl.BlockSpec(memory_space=pltpu.SMEM)
VMEM = pl.BlockSpec(memory_space=pltpu.VMEM)


def cost(nanoseconds):
    return pl.CostEstimate(flops=nanoseconds * 1_000_000, bytes_accessed=1 << 20, transcendentals=0)


def pack_kernel(starts, lengths, x_ref, out_ref, cut_ref):
    for head in range(GROUP):
        for stream in range(3):
            out_ref[head, stream] = x_ref[stream, :, head * HEAD_DIM : (head + 1) * HEAD_DIM]
    long_start = jnp.int32(0)
    for record in range(starts.shape[0]):
        long_start = jnp.where(lengths[record] == LONG, starts[record], long_start)
    cut_ref[0] = lax.rem(long_start // (2 * x_ref.shape[1]) + 1, GROUP)


def pack(starts, lengths, streams):
    rows = streams.shape[1]
    return pl.pallas_call(
        pack_kernel,
        out_shape=(
            jax.ShapeDtypeStruct((GROUP, 3, rows, HEAD_DIM), streams.dtype),
            jax.ShapeDtypeStruct((1,), jnp.int32),
        ),
        in_specs=[SMEM, SMEM, VMEM],
        out_specs=(VMEM, SMEM),
        name="pack_heads",
    )(starts, lengths, streams)


def group_of(cut):
    return lax.rem(lax.axis_index("z") + CHIPS - cut, CHIPS) // GROUP


def attend_rows(q, query_pos, row_start, sources, state):
    rows = q.shape[0]
    scores = []
    for keys, _, first in sources:
        s = lax.dot_general(q, keys, (((1,), (1,)), ((), ())), preferred_element_type=jnp.float32)
        key_pos = jnp.concatenate(
            [here + lax.broadcasted_iota(jnp.int32, (1, rows), 1) for here in first], axis=1
        )
        allowed = (key_pos >= row_start) & (key_pos <= query_pos)
        scores.append(jnp.where(allowed, s * SCALE, MASKED))
    top = functools.reduce(jnp.maximum, [jnp.max(s, axis=1, keepdims=True) for s in scores])
    if state is not None:
        top = jnp.maximum(top, state[0])
    total = jnp.zeros((rows, 1), jnp.float32)
    summed = jnp.zeros((rows, HEAD_DIM), jnp.float32)
    for s, (_, values, _) in zip(scores, sources):
        weights = jnp.exp2(s - top)
        total = total + jnp.sum(weights, axis=1, keepdims=True)
        summed = summed + jnp.dot(
            weights.astype(jnp.bfloat16), values, preferred_element_type=jnp.float32
        )
    if state is not None:
        factor = jnp.exp2(state[0] - top)
        total = total + state[1] * factor
        summed = summed + state[2] * factor
    return top, total, summed


def chip_position(cut, group, place, core, rows):
    chip = lax.rem(group * GROUP + place + (cut + 2 * CHIPS), CHIPS)
    return (chip * 2 + core) * rows


def blocks_of(ref, low, high, offset=0):
    rows = ref.shape[2]
    return [ref[low:high, offset + i].reshape((high - low) * rows, HEAD_DIM) for i in range(2)]


def attend_kernel(cut, phase, starts, q_ref, *refs):
    group, core = group_of(cut), lax.axis_index("core")
    rows = q_ref.shape[2]
    place = lax.broadcasted_iota(jnp.int32, (rows, 1), 0)

    def source(ref, back, of_core, low, high, first=0, offset=0):
        blocks = blocks_of(ref, low, high, offset)
        where = range(first + low, first + high)
        return *blocks, [chip_position(cut, group - back, i, of_core, rows) for i in where]

    for block in range(GROUP):
        query_pos = chip_position(cut, group, block, core, rows) + place
        state = None
        if phase == 0:
            other, *outs = refs
            sources = [
                source(q_ref, 0, core, 0, block + 1, offset=1),
                source(other, 0, 1 - core, 0, block + 1),
            ]
        elif phase == 1:
            before, *state = refs[:4]
            outs = refs[4:]
            sources = [source(before, 1, core, 0, GROUP)]
        else:
            before, far, far_other, *state = refs[:6]
            outs = refs[6:]
            sources = [
                source(before, 1, 1 - core, 0, GROUP),
                source(far, 2, core, 0, 1, first=GROUP - 1),
                source(far_other, 2, 1 - core, 0, 1, first=GROUP - 1),
            ]
        top, total, summed = attend_rows(
            q_ref[block, 0],
            query_pos,
            row_starts(starts, query_pos),
            sources,
            state and [ref[block] for ref in state],
        )
        if phase < 2:
            outs[0][block], outs[1][block], outs[2][block] = top, total, summed
        else:
            outs[0][block] = summed / total


def attend(cut, phase, starts, received, *others):
    rows = received.shape[2]
    column = jax.ShapeDtypeStruct((GROUP, rows, 1), jnp.float32)
    full = jax.ShapeDtypeStruct((GROUP, rows, HEAD_DIM), jnp.float32)
    return pl.pallas_call(
        functools.partial(attend_kernel, cut, phase),
        out_shape=full if phase == 2 else (column, column, full),
        in_specs=[SMEM] + [VMEM] * (1 + len(others)),
        compiler_params=pltpu.CompilerParams(vmem_limit_bytes=32 * 1024 * 1024),
        cost_estimate=cost(2000),
        name=f"attend{phase}",
    )(starts, received, *others)


def row_starts(starts, positions):
    found = jnp.zeros_like(positions)
    for record in range(starts.shape[0]):
        here = starts[record]
        found = jnp.where(positions >= here, here, found)
    return found


def hyena_kernel(starts, residual, streams, rim, taps_ref, out_ref, padded):
    rows = residual.shape[0]
    edge = rim.shape[1]
    taps = taps_ref.shape[0]
    positions = lax.axis_index(POSITIONS) * rows + lax.broadcasted_iota(jnp.int32, (rows, 1), 0)
    first = row_starts(starts, positions)
    padded[:edge] = rim[0].astype(jnp.float32) * rim[1].astype(jnp.float32)
    padded[edge:] = streams[1].astype(jnp.float32) * streams[2].astype(jnp.float32)
    filtered = jnp.zeros(out_ref.shape, jnp.float32)
    for tap in range(taps):
        term = taps_ref[tap : tap + 1, :] * padded[edge - tap : edge - tap + rows]
        filtered = filtered + jnp.where(positions - tap >= first, term, 0.0)
    out_ref[...] = residual[...].astype(jnp.float32) + streams[0].astype(jnp.float32) * filtered


def stream_kernel(base, heads, stream_ref, squares_ref):
    rows = base.shape[0]
    squares = jnp.zeros((rows, HEAD_DIM), jnp.float32)
    for head in range(GROUP):
        columns = slice(head * HEAD_DIM, (head + 1) * HEAD_DIM)
        value = base[:, columns] + heads[head]
        stream_ref[:, columns] = value
        squares = squares + value * value
    line = jnp.sum(squares.T, axis=0, keepdims=True)
    for device in range(squares_ref.shape[0]):
        squares_ref[device] = line


def records_kernel(starts, lengths, parts, mean_ref, sums_ref):
    rows = parts.shape[2]
    line = jnp.sum(parts[:, 0, :], axis=0, keepdims=True) / D
    mean = jnp.broadcast_to(line, (rows, rows)).T
    mean_ref[...] = mean
    position = lax.axis_index(POSITIONS) * rows + lax.broadcasted_iota(jnp.int32, (rows, rows), 0)
    first = starts[...]
    inside = (position >= first) & (position < first + lengths[...])
    sums = jnp.sum(jnp.where(inside, mean, 0.0), axis=0, keepdims=True)
    for device in range(sums_ref.shape[0]):
        sums_ref[device] = sums


def scale_kernel(stream, mean, gain, out_ref):
    factor = lax.rsqrt(mean[...] + 1e-05)
    for head in range(GROUP):
        columns = slice(head * HEAD_DIM, (head + 1) * HEAD_DIM)
        out_ref[:, columns] = stream[:, columns] * factor * gain[:, columns]


def mixers(cut, packed, residual, streams, taps, starts):
    rows, width = residual.shape
    seq = lax.axis_size(POSITIONS)
    groups = [
        [(cut + GROUP * k + i) % CHIPS for i in range(GROUP)] for k in range(CHIPS // GROUP)
    ]
    swap = [(0, 1), (1, 0)]

    def along(value, chips, of_groups):
        pairs = [(i, (i + chips) % CHIPS) for k in of_groups for i in groups[k]]
        return lax.ppermute(value, "z", pairs)

    last = [3] if cut else []
    rim = lax.ppermute(streams[1:, rows - 16 :], POSITIONS, [(i, i + 1) for i in range(seq - 1)])
    received = lax.all_to_all(packed, "z", 0, 0, axis_index_groups=groups, tiled=True)
    far = along(received[GROUP - 1 :, 1:], 2 * GROUP, [0, 1] + last)
    key_value, rim = lax.optimization_barrier((received[:, 1:], rim))
    before = along(key_value, GROUP, [0, 1, 2] + last)
    other = lax.ppermute(key_value, "core", swap)
    base = pl.pallas_call(
        hyena_kernel,
        out_shape=jax.ShapeDtypeStruct((rows, width), jnp.float32),
        in_specs=[SMEM, VMEM, VMEM, VMEM, VMEM],
        out_specs=VMEM,
        scratch_shapes=[pltpu.VMEM((rows + 16, width), jnp.float32)],
        cost_estimate=cost(2000),
        name="hyena",
    )(starts, residual, streams, rim, taps)
    state = attend(cut, 0, starts, received, other)
    before, far, base, state = lax.optimization_barrier((before, far, base, state))
    before_other = lax.ppermute(before, "core", swap)
    far_other = lax.ppermute(far, "core", swap)
    state = attend(cut, 1, starts, received, before, *state)
    out = attend(cut, 2, starts, received, before_other, far, far_other, *state)
    heads = lax.all_to_all(out, "z", 0, 0, axis_index_groups=groups, tiled=True)
    return base, heads


def on_device(
    residual,
    hyena_streams,
    hyena_filter,
    attention_streams,
    norm_gain,
    record_starts,
    record_lengths,
    segment_ids,
):
    rows, width = residual.shape
    records = record_starts.shape[0]
    seq, mp = lax.axis_size(POSITIONS), lax.axis_size("mp")
    packed, cut = pack(record_starts, record_lengths, attention_streams.transpose(1, 0, 2))
    base, heads = lax.switch(
        cut[0],
        [functools.partial(mixers, here) for here in range(GROUP)],
        packed,
        residual,
        hyena_streams.transpose(1, 0, 2),
        hyena_filter,
        record_starts,
    )

    with jax.named_scope("mean_square"):
        stream, squares = pl.pallas_call(
            stream_kernel,
            out_shape=(
                jax.ShapeDtypeStruct((rows, width), jnp.float32),
                jax.ShapeDtypeStruct((mp, 1, rows), jnp.float32),
            ),
            name="stream",
        )(base, heads)
        parts = lax.all_to_all(squares, "mp", 0, 0, tiled=True)
    with jax.named_scope("record_energy"):
        lines = [jnp.pad(x, (0, 128 - records))[None, :] for x in (record_starts, record_lengths)]
        mean, sums = pl.pallas_call(
            records_kernel,
            out_shape=(
                jax.ShapeDtypeStruct((rows, rows), jnp.float32),
                jax.ShapeDtypeStruct((seq, 1, 128), jnp.float32),
            ),
            name="records",
        )(*lines, parts)
        sums = lax.all_to_all(sums, POSITIONS, 0, 0, tiled=True)
        record_energy = jnp.sum(sums, axis=(0, 1))[:records] / record_lengths.astype(jnp.float32)
    mixed = pl.pallas_call(
        scale_kernel,
        out_shape=jax.ShapeDtypeStruct((rows, width), jnp.float32),
        cost_estimate=cost(1000),
        name="scale",
    )(stream, mean, norm_gain[None, :])
    return (mixed, record_energy)


def solution(mesh):
    fine = Mesh(mesh.devices.reshape(CHIPS, 2, mesh.shape["mp"]), ("z", "core", "mp"))
    return jax.shard_map(
        on_device,
        mesh=fine,
        in_specs=(
            P(POSITIONS, "mp"),
            P(POSITIONS, None, "mp"),
            P(None, "mp"),
            P(POSITIONS, None, "mp"),
            P("mp"),
            P(),
            P(),
            P(POSITIONS),
        ),
        out_specs=(P(POSITIONS, "mp"), P()),
        check_vma=False,
    )
```

time: 142 us -> 129 us (0.908)
  waiting for transfers between devices: 47.1 us -> 42.9 us
  starting transfers between devices: 58.2 us -> 55.8 us
  other arithmetic: 2.53 us -> 0.57 us
  between operations: 3.3 us -> 1.34 us
  blocking collectives: 13.8 us -> 12 us
    ppermute x3, waiting for transfers between devices: 25.2 us -> 20.2 us  [the longest x2 20.2 us: along(): return lax.ppermute(value, 'z', pairs)]
    ppermute x3, starting transfers between devices: 17.1 us -> 14.1 us  [the longest x2 12.2 us: along(): return lax.ppermute(value, 'z', pairs)]
    all_to_all x1, blocking collectives: 13.8 us -> 12 us  [mixers(): heads = lax.all_to_all(out, 'z', 0, 0, axis_index_groups=groups, tiled=True)]
  transfers between devices with their start and end apart: 9 -> 9, of which waited for: 5 -> 4; matrix products, arithmetic and copies ran while one was open for 1% -> 0% of each run, Pallas kernels for 5% -> 6%
where the time goes in v4:
time: 129 us; the launch traced here: 128 us
  starting transfers between devices  55.8 us (43%)
  waiting for transfers between devices  42.9 us (33%)
  Pallas kernels  13.8 us (11%)
  blocking collectives  12 us (9%)
  local copies, waits for them, and re-layouts  1.83 us (1%)
  between operations  1.34 us (1%)
    ppermute x2, waiting for transfers between devices, along(): return lax.ppermute(value, 'z', pairs)  20.2 us
    all_to_all x1, starting transfers between devices, mixers(): lax.all_to_all(packed, 'z', 0, 0, axis_index_groups=groups, tiled=True)  14.4 us
    ppermute x2, starting transfers between devices, along(): return lax.ppermute(value, 'z', pairs)  12.2 us
    all_to_all x1, blocking collectives, mixers(): heads = lax.all_to_all(out, 'z', 0, 0, axis_index_groups=groups, tiled=True)  12 us
    all_to_all x1, starting transfers between devices, on_device(): sums = lax.all_to_all(sums, POSITIONS, 0, 0, tiled=True)  11.9 us
    all_to_all x1, waiting for transfers between devices, on_device(): sums = lax.all_to_all(sums, POSITIONS, 0, 0, tiled=True)  10 us
    all_to_all x1, starting transfers between devices, on_device(): parts = lax.all_to_all(squares, 'mp', 0, 0, tiled=True)  6.88 us
    all_to_all x1, waiting for transfers between devices, mixers(): lax.all_to_all(packed, 'z', 0, 0, axis_index_groups=groups, tiled=True)  6.85 us
  transfers between devices with their start and end apart: 9, of which 4 were waited for; matrix products, arithmetic and copies ran while one was open for 0% of the time, Pallas kernels for 6%

profile of v4, /device:TPU:1, one launch (start us, length us, event | category | flops | bytes accessed | tf_op | source)
XLA Modules:
  0.0 128.4 jit_solution(4728446384811618819)
XLA Ops:
  0.6 0.0 copy-start.2
  0.6 0.0 copy-start
  0.7 0.6 copy-done.2
  1.3 1.8 %pack_heads.1 = (bf16[4,3,128,128]{3,2,1,0:T(8,128)(2,1)}, s32[1]{0:T(128)}) custom-call(s32[16]{0:T(128)S(1)} %copy-done.2, s32[16]{0:T(128)} %lengths.1, bf16[3,128,512]{2,1,0:T(8,128)(2,1)} %bitcast.8), custom_call_target="tpu_custom_call" | custom-call | tf_op jit(solution)/shard_map/pack_heads/pallas_call | solution.py:39
  3.8 0.0 copy-done
  3.8 84.3 %conditional.1 = (f32[128,512]{1,0:T(8,128)S(1)}, f32[4,128,128]{2,1,0:T(8,128)S(1)}) conditional(s32[]{:T(128)} %bitcast.1, (bf16[4,3,128,128]{3,2,1,0:T(8,128)(2,1)}, bf16[3,128,512]{2,1,0:T(8,128)(2,1)S(1)}, s32[16]{0:T(128)S(1)}, bf16[128,512]{1,0:T(8,128)(2,1)}, f32[7,512]{1,0:T(8,128)}) %tuple.43, ...), branch_computations={%region_0.0_spmd, %region_1.0_spmd, %region_2.0_spmd, %region_3.0_... | conditional | flops 8000000000 | bytes 11133300 | solution.py:259
  3.8 14.4 %all-to-all-start.2 = ((bf16[4,3,128,128]{3,2,1,0:T(8,128)(2,1)}), bf16[4,3,128,128]{3,2,1,0:T(8,128)(2,1)S(1)}, u32[]{:S(2)}, u32[]{:S(2)}) async-start(bf16[4,3,128,128]{3,2,1,0:T(8,128)(2,1)} %get-tuple-element.59), calls=%async_computation.2 | async-start | bytes 786432 | tf_op jit(solution)/shard_map/cond/branch_1_fun/all_to_all | solution.py:221
  18.2 1.9 %collective-permute-start.6 = (bf16[2,16,512]{2,1,0:T(8,128)(2,1)S(1)}, bf16[2,16,512]{2,1,0:T(8,128)(2,1)S(1)}, u32[]{:S(2)}, u32[]{:S(2)}) collective-permute-start(bf16[2,16,512]{2,1,0:T(8,128)(2,1)S(1)} %slice.30), channel_id=1, source_target_pairs={{0,16},{16,32},{32,48},{48,64},{64,80},{80,96},{96,112},{112,128},... | collective-permute-start | bytes 98312 | tf_op jit(solution)/shard_map/cond/branch_1_fun/ppermute | solution.py:220
  20.1 6.8 %all-to-all-done.2.q_ref = bf16[4,3,128,128]{3,2,1,0:T(8,128)(2,1)S(1)} async-done(((bf16[4,3,128,128]{3,2,1,0:T(8,128)(2,1)}), bf16[4,3,128,128]{3,2,1,0:T(8,128)(2,1)S(1)}, u32[]{:S(2)}, u32[]{:S(2)}) %all-to-all-start.2) | async-done | bytes 393248 | tf_op jit(solution)/shard_map/cond/branch_1_fun/all_to_all | solution.py:221
  27.0 0.0 copy-start.13
  27.0 0.0 copy-start.5
  27.0 0.0 collective-permute-done.6.rim
  27.0 0.0 copy-start.9
  27.0 4.2 %collective-permute-start.9 = (bf16[4,2,128,128]{3,2,1,0:T(8,128)(2,1)S(1)}, bf16[4,2,128,128]{3,2,1,0:T(8,128)(2,1)S(1)}, u32[]{:S(2)}, u32[]{:S(2)}) collective-permute-start(bf16[4,2,128,128]{3,2,1,0:T(8,128)(2,1)S(1)} %slice.42), channel_id=1, source_target_pairs={{0,16},{16,0},{1,17},{17,1},{2,18},{18,2},{3,19},{19,3},{4,20},{20... | collective-permute-start | bytes 786440 | tf_op jit(solution)/shard_map/cond/branch_1_fun/ppermute | solution.py:225
  31.2 1.9 %collective-permute-start.7 = (bf16[4,2,128,128]{3,2,1,0:T(8,128)(2,1)S(1)}, bf16[4,2,128,128]{3,2,1,0:T(8,128)(2,1)S(1)}, u32[]{:S(2)}, u32[]{:S(2)}) collective-permute-start(bf16[4,2,128,128]{3,2,1,0:T(8,128)(2,1)S(1)} %slice.42), channel_id=1, source_target_pairs={{32,160},{64,192},{96,224},{128,256},{160,288},{192,320},{224,352}... | collective-permute-start | bytes 786440 | tf_op jit(solution)/shard_map/cond/branch_1_fun/ppermute | solution.py:217
  33.1 0.0 copy-done.9
  33.2 10.3 %collective-permute-start.8 = (bf16[1,2,128,128]{3,2,1,0:T(8,128)(2,1)S(1)}, bf16[1,2,128,128]{3,2,1,0:T(8,128)(2,1)S(1)}, u32[]{:S(2)}, u32[]{:S(2)}) collective-permute-start(bf16[1,2,128,128]{3,2,1,0:T(8,128)(2,1)S(1)} %slice.43), channel_id=1, source_target_pairs={{32,288},{64,320},{96,352},{128,384},{160,416},{192,448},{224,480}... | collective-permute-start | bytes 196616 | tf_op jit(solution)/shard_map/cond/branch_1_fun/ppermute | solution.py:217
  43.4 0.0 copy-done.13
  43.4 0.0 copy-done.5
  43.4 1.3 %hyena.5 = f32[128,512]{1,0:T(8,128)S(1)} custom-call(s32[16]{0:T(128)S(1)} %get-tuple-element.62.starts, bf16[128,512]{1,0:T(8,128)(2,1)S(1)} %copy-done.5, bf16[3,128,512]{2,1,0:T(8,128)(2,1)S(1)} %get-tuple-element.60.streams, bf16[2,16,512]{2,1,0:T(8,128)(2,1)} %copy-done.9, f32[7,512]{1,0:T(8,128)S(1)} %copy-done.13), custom_call_target="tpu_custom_call" | custom-call | flops 2000000000 | bytes 1048576 | tf_op jit(solution)/shard_map/cond/branch_1_fun/hyena/pallas_call | solution.py:226
  44.8 0.0 collective-permute-done.9.refs_0_
  44.8 1.9 %attend0.5 = (f32[4,128,1]{2,1,0:T(8,128)S(1)}, f32[4,128,1]{2,1,0:T(8,128)S(1)}, f32[4,128,128]{2,1,0:T(8,128)S(1)}) custom-call(s32[16]{0:T(128)S(1)} %get-tuple-element.62.starts, bf16[4,3,128,128]{3,2,1,0:T(8,128)(2,1)S(1)} %all-to-all-done.2.q_ref, bf16[4,2,128,128]{3,2,1,0:T(8,128)(2,1)S(1)} %collective-permute-done.9.refs_0_), custom_call_target="tpu_custom_call" | custom-call | flops 2000000000 | bytes 1048576 | tf_op jit(solution)/shard_map/cond/branch_1_fun/attend0/pallas_call | solution.py:141
  46.7 20.2 %collective-permute-done.8.refs_1_ = bf16[1,2,128,128]{3,2,1,0:T(8,128)(2,1)S(1)} collective-permute-done((bf16[1,2,128,128]{3,2,1,0:T(8,128)(2,1)S(1)}, bf16[1,2,128,128]{3,2,1,0:T(8,128)(2,1)S(1)}, u32[]{:S(2)}, u32[]{:S(2)}) %collective-permute-start.8) | collective-permute-done | bytes 65568 | tf_op jit(solution)/shard_map/cond/branch_1_fun/ppermute | solution.py:217
  67.0 0.0 collective-permute-done.7.refs_0_
  67.0 2.4 %collective-permute-start.10 = (bf16[4,2,128,128]{3,2,1,0:T(8,128)(2,1)S(1)}, bf16[4,2,128,128]{3,2,1,0:T(8,128)(2,1)S(1)}, u32[]{:S(2)}, u32[]{:S(2)}) collective-permute-start(bf16[4,2,128,128]{3,2,1,0:T(8,128)(2,1)S(1)} %collective-permute-done.7.refs_0_), channel_id=1, source_target_pairs={{0,16},{16,0},{1,17},{17,1},{2,18},{18,2},{3,19},{19,3},{4,20},{20... | collective-permute-start | bytes 786440 | tf_op jit(solution)/shard_map/cond/branch_1_fun/ppermute | solution.py:237
  69.4 1.9 %collective-permute-start.11 = (bf16[1,2,128,128]{3,2,1,0:T(8,128)(2,1)S(1)}, bf16[1,2,128,128]{3,2,1,0:T(8,128)(2,1)S(1)}, u32[]{:S(2)}, u32[]{:S(2)}) collective-permute-start(bf16[1,2,128,128]{3,2,1,0:T(8,128)(2,1)S(1)} %collective-permute-done.8.refs_1_), channel_id=1, source_target_pairs={{0,16},{16,0},{1,17},{17,1},{2,18},{18,2},{3,19},{19,3},{4,20},{20... | collective-permute-start | bytes 196616 | tf_op jit(solution)/shard_map/cond/branch_1_fun/ppermute | solution.py:238
  71.3 2.1 %attend1.5 = (f32[4,128,1]{2,1,0:T(8,128)S(1)}, f32[4,128,1]{2,1,0:T(8,128)S(1)}, f32[4,128,128]{2,1,0:T(8,128)S(1)}) custom-call(s32[16]{0:T(128)S(1)} %get-tuple-element.62.starts, bf16[4,3,128,128]{3,2,1,0:T(8,128)(2,1)S(1)} %all-to-all-done.2.q_ref, bf16[4,2,128,128]{3,2,1,0:T(8,128)(2,1)S(1)} %collective-permute-done.7.refs_0_, ...), custom_call_target="tpu_custom_call" | custom-call | flops 2000000000 | bytes 1048576 | tf_op jit(solution)/shard_map/cond/branch_1_fun/attend1/pallas_call | solution.py:141
  73.5 0.0 collective-permute-done.11.refs_2_
  73.5 0.0 collective-permute-done.10.refs_0_
  73.5 2.6 %attend2.5 = f32[4,128,128]{2,1,0:T(8,128)S(1)} custom-call(s32[16]{0:T(128)S(1)} %get-tuple-element.62.starts, bf16[4,3,128,128]{3,2,1,0:T(8,128)(2,1)S(1)} %all-to-all-done.2.q_ref, bf16[4,2,128,128]{3,2,1,0:T(8,128)(2,1)S(1)} %collective-permute-done.10.refs_0_, bf16[1,2,128,128]{3,2,1,0:T(8,128)(2,1)S(1)} %collective-permute-done.8.refs_1_, ...), custom_call_target="tpu_custom_call" | custom-call | flops 2000000000 | bytes 1048576 | tf_op jit(solution)/shard_map/cond/branch_1_fun/attend2/pallas_call | solution.py:141
  76.1 12.0 %all_to_all.43 = f32[4,128,128]{2,1,0:T(8,128)S(1)} all-to-all(f32[4,128,128]{2,1,0:T(8,128)S(1)} %attend2.5), channel_id=1, replica_groups={{32,64,96,128},{160,192,224,256},{288,320,352,384},{416,448,480,0},{33,..., dimensions={0} | all-to-all | bytes 524288 | tf_op jit(solution)/shard_map/cond/branch_1_fun/all_to_all | solution.py:241
  88.1 0.7 stream.1
  88.8 0.0 copy-start.3
  88.8 6.9 %all-to-all-start.8 = ((f32[16,1,128]{2,1,0:T(1,128)}), f32[16,1,128]{2,1,0:T(1,128)S(1)}, u32[]{:S(2)}, u32[]{:S(2)}) async-start(f32[16,1,128]{2,1,0:T(1,128)} %get-tuple-element.131), calls=%async_computation.8 | async-start | bytes 16384 | tf_op jit(solution)/shard_map/mean_square/all_to_all | solution.py:278
  95.7 0.0 copy-done.3
  95.8 0.5 pad_bitcast_fusion
  96.3 5.8 %all-to-all-done.8.parts = f32[16,1,128]{2,1,0:T(1,128)S(1)} async-done(((f32[16,1,128]{2,1,0:T(1,128)}), f32[16,1,128]{2,1,0:T(1,128)S(1)}, u32[]{:S(2)}, u32[]{:S(2)}) %all-to-all-start.8) | async-done | bytes 8224 | tf_op jit(solution)/shard_map/mean_square/all_to_all | solution.py:278
  102.1 0.0 copy-start.1
  102.1 0.6 copy-done.1
  102.7 1.5 %records.1 = (f32[128,128]{1,0:T(8,128)}, f32[32,1,128]{2,1,0:T(1,128)}) custom-call(s32[1,128]{1,0:T(1,128)} %get-tuple-element.135.starts, s32[1,128]{1,0:T(1,128)} %get-tuple-element.134.lengths, f32[16,1,128]{2,1,0:T(1,128)} %copy-done.1), custom_call_target="tpu_custom_call" | custom-call | tf_op jit(solution)/shard_map/record_energy/records/pallas_call | solution.py:281
  104.1 11.9 %all-to-all-start.9 = ((f32[32,1,128]{2,1,0:T(1,128)}), f32[32,1,128]{2,1,0:T(1,128)S(1)}, u32[]{:S(2)}, u32[]{:S(2)}) async-start(f32[32,1,128]{2,1,0:T(1,128)} %get-tuple-element.133), calls=%async_computation.9 | async-start | bytes 32768 | tf_op jit(solution)/shard_map/record_energy/all_to_all | solution.py:289
  116.0 1.7 %scale.1 = f32[128,512]{1,0:T(8,128)} custom-call(f32[128,512]{1,0:T(8,128)} %get-tuple-element.130.stream, f32[128,128]{1,0:T(8,128)} %get-tuple-element.132.mean, f32[1,512]{1,0:T(1,128)} %bitcast.13), custom_call_target="tpu_custom_call" | custom-call | flops 1000000000 | bytes 1048576 | tf_op jit(solution)/shard_map/scale/pallas_call | solution.py:291
  117.8 10.0 %all-to-all-done.9 = f32[32,1,128]{2,1,0:T(1,128)S(1)} async-done(((f32[32,1,128]{2,1,0:T(1,128)}), f32[32,1,128]{2,1,0:T(1,128)S(1)}, u32[]{:S(2)}, u32[]{:S(2)}) %all-to-all-start.9) | async-done | bytes 16416 | tf_op jit(solution)/shard_map/record_energy/all_to_all | solution.py:289
  127.8 0.1 reduce_sum.9
  127.8 0.5 convert_divide_fusion
  (3 shorter events, 0.0 us)
Async XLA Ops:
  0.6 0.7 copy-start.2
  0.6 3.1 %copy-start = (bf16[128,3,512]{2,0,1:T(8,128)(2,1)S(1)}, bf16[128,3,512]{2,0,1:T(8,128)(2,1)}, u32[]{:S(2)}) copy-start(bf16[128,3,512]{2,0,1:T(8,128)(2,1)} %param.13) | copy-start | bytes 1179652
  3.8 23.1 %all-to-all-start.2 = ((bf16[4,3,128,128]{3,2,1,0:T(8,128)(2,1)}), bf16[4,3,128,128]{3,2,1,0:T(8,128)(2,1)S(1)}, u32[]{:S(2)}, u32[]{:S(2)}) async-start(bf16[4,3,128,128]{3,2,1,0:T(8,128)(2,1)} %get-tuple-element.59), calls=%async_computation.2 | async-start | bytes 786432 | tf_op jit(solution)/shard_map/cond/branch_1_fun/all_to_all | solution.py:221
  18.2 8.8 %collective-permute-start.6 = (bf16[2,16,512]{2,1,0:T(8,128)(2,1)S(1)}, bf16[2,16,512]{2,1,0:T(8,128)(2,1)S(1)}, u32[]{:S(2)}, u32[]{:S(2)}) collective-permute-start(bf16[2,16,512]{2,1,0:T(8,128)(2,1)S(1)} %slice.30), channel_id=1, source_target_pairs={{0,16},{16,32},{32,48},{48,64},{64,80},{80,96},{96,112},{112,128},... | collective-permute-start | bytes 98312 | tf_op jit(solution)/shard_map/cond/branch_1_fun/ppermute | solution.py:220
  27.0 16.5 %copy-start.13 = (f32[7,512]{1,0:T(8,128)S(1)}, f32[7,512]{1,0:T(8,128)}, u32[]{:S(2)}) copy-start(f32[7,512]{1,0:T(8,128)} %get-tuple-element.65.taps_ref) | copy-start | bytes 43012 | tf_op jit(solution)/shard_map/cond
  27.0 16.4 %copy-start.5 = (bf16[128,512]{1,0:T(8,128)(2,1)S(1)}, bf16[128,512]{1,0:T(8,128)(2,1)}, u32[]{:S(2)}) copy-start(bf16[128,512]{1,0:T(8,128)(2,1)} %get-tuple-element.63.residual) | copy-start | bytes 393220 | tf_op jit(solution)/shard_map/cond
  27.0 6.1 %copy-start.9 = (bf16[2,16,512]{2,1,0:T(8,128)(2,1)}, bf16[2,16,512]{2,1,0:T(8,128)(2,1)S(1)}, u32[]{:S(2)}) copy-start(bf16[2,16,512]{2,1,0:T(8,128)(2,1)S(1)} %collective-permute-done.6.rim) | copy-start | bytes 98308 | tf_op jit(solution)/shard_map/cond
  27.0 17.8 %collective-permute-start.9 = (bf16[4,2,128,128]{3,2,1,0:T(8,128)(2,1)S(1)}, bf16[4,2,128,128]{3,2,1,0:T(8,128)(2,1)S(1)}, u32[]{:S(2)}, u32[]{:S(2)}) collective-permute-start(bf16[4,2,128,128]{3,2,1,0:T(8,128)(2,1)S(1)} %slice.42), channel_id=1, source_target_pairs={{0,16},{16,0},{1,17},{17,1},{2,18},{18,2},{3,19},{19,3},{4,20},{20... | collective-permute-start | bytes 786440 | tf_op jit(solution)/shard_map/cond/branch_1_fun/ppermute | solution.py:225
  31.2 35.8 %collective-permute-start.7 = (bf16[4,2,128,128]{3,2,1,0:T(8,128)(2,1)S(1)}, bf16[4,2,128,128]{3,2,1,0:T(8,128)(2,1)S(1)}, u32[]{:S(2)}, u32[]{:S(2)}) collective-permute-start(bf16[4,2,128,128]{3,2,1,0:T(8,128)(2,1)S(1)} %slice.42), channel_id=1, source_target_pairs={{32,160},{64,192},{96,224},{128,256},{160,288},{192,320},{224,352}... | collective-permute-start | bytes 786440 | tf_op jit(solution)/shard_map/cond/branch_1_fun/ppermute | solution.py:217
  33.2 33.8 %collective-permute-start.8 = (bf16[1,2,128,128]{3,2,1,0:T(8,128)(2,1)S(1)}, bf16[1,2,128,128]{3,2,1,0:T(8,128)(2,1)S(1)}, u32[]{:S(2)}, u32[]{:S(2)}) collective-permute-start(bf16[1,2,128,128]{3,2,1,0:T(8,128)(2,1)S(1)} %slice.43), channel_id=1, source_target_pairs={{32,288},{64,320},{96,352},{128,384},{160,416},{192,448},{224,480}... | collective-permute-start | bytes 196616 | tf_op jit(solution)/shard_map/cond/branch_1_fun/ppermute | solution.py:217
  67.0 6.5 %collective-permute-start.10 = (bf16[4,2,128,128]{3,2,1,0:T(8,128)(2,1)S(1)}, bf16[4,2,128,128]{3,2,1,0:T(8,128)(2,1)S(1)}, u32[]{:S(2)}, u32[]{:S(2)}) collective-permute-start(bf16[4,2,128,128]{3,2,1,0:T(8,128)(2,1)S(1)} %collective-permute-done.7.refs_0_), channel_id=1, source_target_pairs={{0,16},{16,0},{1,17},{17,1},{2,18},{18,2},{3,19},{19,3},{4,20},{20... | collective-permute-start | bytes 786440 | tf_op jit(solution)/shard_map/cond/branch_1_fun/ppermute | solution.py:237
  69.4 4.1 %collective-permute-start.11 = (bf16[1,2,128,128]{3,2,1,0:T(8,128)(2,1)S(1)}, bf16[1,2,128,128]{3,2,1,0:T(8,128)(2,1)S(1)}, u32[]{:S(2)}, u32[]{:S(2)}) collective-permute-start(bf16[1,2,128,128]{3,2,1,0:T(8,128)(2,1)S(1)} %collective-permute-done.8.refs_1_), channel_id=1, source_target_pairs={{0,16},{16,0},{1,17},{17,1},{2,18},{18,2},{3,19},{19,3},{4,20},{20... | collective-permute-start | bytes 196616 | tf_op jit(solution)/shard_map/cond/branch_1_fun/ppermute | solution.py:238
  88.8 6.9 %copy-start.3 = (s32[16]{0:T(128)S(1)}, s32[16]{0:T(128)}, u32[]{:S(2)}) copy-start(s32[16]{0:T(128)} %lengths.1) | copy-start | bytes 196
  88.8 13.2 %all-to-all-start.8 = ((f32[16,1,128]{2,1,0:T(1,128)}), f32[16,1,128]{2,1,0:T(1,128)S(1)}, u32[]{:S(2)}, u32[]{:S(2)}) async-start(f32[16,1,128]{2,1,0:T(1,128)} %get-tuple-element.131), calls=%async_computation.8 | async-start | bytes 16384 | tf_op jit(solution)/shard_map/mean_square/all_to_all | solution.py:278
  102.1 0.6 copy-start.1
  104.1 23.6 %all-to-all-start.9 = ((f32[32,1,128]{2,1,0:T(1,128)}), f32[32,1,128]{2,1,0:T(1,128)S(1)}, u32[]{:S(2)}, u32[]{:S(2)}) async-start(f32[32,1,128]{2,1,0:T(1,128)} %get-tuple-element.133), calls=%async_computation.9 | async-start | bytes 32768 | tf_op jit(solution)/shard_map/record_energy/all_to_all | solution.py:289
